TPU v7x, 512 devices: a whole 4x8x8 slice. The times are simulated.
512 devices in a mesh: pipe: 32 (over y_lo, z), dp: 8 (over x, y_hi), mp: 2 (over core).
Axes of the slice: x: 4, y: 8 (y_hi: 2, y_lo: 4; y = y_hi * 4 + y_lo), z: 8, core: 2. Of those that a mesh axis runs over, the one named last changes fastest.
Arguments:
- activations: bfloat16 [8, 128, 7168], P('dp', 'pipe', 'mp'), may hold values from -6 to 6
- cotangent: bfloat16 [8, 128, 7168], P('dp', 'pipe', 'mp'), may hold values from -6 to 6
- squeeze_old: bfloat16 [32, 7168, 64], P('pipe', 'mp'), may hold values from -5 to 5
- expand_old: bfloat16 [32, 64, 7168], P('pipe', None, 'mp'), may hold values from -5 to 5
- squeeze_late: bfloat16 [8, 32, 7168, 64], P('dp', 'pipe', 'mp'), may hold values from -6 to 6
- expand_late: bfloat16 [8, 32, 64, 7168], P('dp', 'pipe', None, 'mp'), may hold values from -6 to 6
- stash_inputs: bfloat16 [8, 32, 8, 16, 7168], P('dp', 'pipe', None, None, 'mp'), may hold values from -6 to 6
- forward_in: bfloat16 [8, 32, 16, 7168], P('dp', 'pipe', None, 'mp'), may hold values from -6 to 6
- backward_in: bfloat16 [8, 32, 16, 7168], P('dp', 'pipe', None, 'mp'), may hold values from -6 to 6
Outputs:
- squeeze_new: bfloat16 [32, 7168, 64], P('pipe', 'mp')
- expand_new: bfloat16 [32, 64, 7168], P('pipe', None, 'mp')
- squeeze_grad: bfloat16 [8, 32, 7168, 64], P('dp', 'pipe', 'mp')
- expand_grad: bfloat16 [8, 32, 64, 7168], P('dp', 'pipe', None, 'mp')
- forward_carry: bfloat16 [8, 32, 16, 7168], P('dp', 'pipe', None, 'mp')
- backward_carry: bfloat16 [8, 32, 16, 7168], P('dp', 'pipe', None, 'mp')
All inputs are finite; a program needn't handle non-finite values.
Results may differ from a plain program's by a relative error of at most 0.009.
Values may be sent and summed in bfloat16 or wider, within the bound.
A program may use at most 64 MiB of HBM per device.

v0:
```python
import math

import jax
import jax.numpy as jnp
from jax import lax
from jax.sharding import PartitionSpec as P

D = 7168
RANK = 64


BRANCH_SCALE = 0.25
STEP_RATE = 0.5


def passed_along(block, axis, distance):
    devices = range(lax.axis_size(axis))
    route = [(i - distance, i) for i in devices if i - distance in devices]
    return lax.ppermute(block, axis, route)


def activate(values):
    return jax.nn.gelu(values, approximate=True)


def shards(
    activations,
    cotangent,
    squeeze_old,
    expand_old,
    squeeze_late,
    expand_late,
    stash_inputs,
    forward_in,
    backward_in,
):
    sections = lax.axis_size("pipe")
    section_index = lax.axis_index("pipe")
    replicas = lax.axis_size("dp")
    squeeze = squeeze_old[0]
    expand = expand_old[0]
    ticks = stash_inputs.shape[2]
    rows = stash_inputs.shape[3]
    inv_width = 1.0 / math.sqrt(D)
    inv_rank = BRANCH_SCALE / math.sqrt(RANK)
    total_squeeze, total_expand = (
        lax.psum(squeeze_late[0, 0].astype(jnp.float32).astype(jnp.bfloat16), "dp").astype(
            jnp.float32
        ),
        lax.psum(expand_late[0, 0].astype(jnp.float32).astype(jnp.bfloat16), "dp").astype(
            jnp.float32
        ),
    )
    squeeze_new = (squeeze.astype(jnp.float32) - STEP_RATE * total_squeeze / replicas).astype(
        jnp.bfloat16
    )
    expand_new = (expand.astype(jnp.float32) - STEP_RATE * total_expand / replicas).astype(
        jnp.bfloat16
    )
    feed_all, target_all = (
        lax.all_gather(activations, "pipe", axis=1, tiled=True),
        lax.all_gather(cotangent, "pipe", axis=1, tiled=True),
    )
    feed_rows = feed_all[0]
    target_rows = target_all[0]
    stash = stash_inputs[0, 0]
    is_first = section_index == 0
    is_last = section_index == sections - 1
    lag = 2 * sections - 1 - 2 * section_index
    incoming_fwd = forward_in[0, 0]
    incoming_bwd = backward_in[0, 0]
    squeeze_sum = jnp.zeros(squeeze.shape, jnp.float32)
    expand_sum = jnp.zeros(expand.shape, jnp.float32)
    history = []
    layer_out = incoming_fwd
    downstream = incoming_bwd
    for tick in range(ticks):
        fed = feed_rows[tick * rows : (tick + 1) * rows]
        target = target_rows[tick * rows : (tick + 1) * rows]
        layer_in = jnp.where(is_first, fed, incoming_fwd)
        upstream = jnp.where(is_last, target, incoming_bwd)
        history.append(layer_in)
        stacked = jnp.stack(history)
        back = tick - lag
        picked = lax.dynamic_index_in_dim(stacked, jnp.clip(back, 0, tick), 0, keepdims=False)
        saved = jnp.where(back >= 0, picked, stash[tick])
        forward_partial = jnp.dot(layer_in, squeeze, preferred_element_type=jnp.float32)
        again_partial = jnp.dot(saved, squeeze, preferred_element_type=jnp.float32)
        grad_partial = lax.dot_general(
            upstream, expand, (((1,), (1,)), ((), ())), preferred_element_type=jnp.float32
        )
        hidden_total = lax.psum(forward_partial, "mp")
        again_total, grad_total = lax.psum((again_partial, grad_partial), "mp")
        hidden = hidden_total * inv_width
        gated = activate(hidden).astype(jnp.bfloat16)
        layer_out = (
            layer_in.astype(jnp.float32)
            + jnp.dot(gated, expand, preferred_element_type=jnp.float32) * inv_rank
        ).astype(jnp.bfloat16)
        again = again_total * inv_width
        gate_grad = grad_total * inv_rank
        regated, pullback = jax.vjp(activate, again)
        hidden_grad = pullback(gate_grad)[0].astype(jnp.bfloat16)
        regated = regated.astype(jnp.bfloat16)
        downstream = (
            upstream.astype(jnp.float32)
            + lax.dot_general(
                hidden_grad, squeeze, (((1,), (1,)), ((), ())), preferred_element_type=jnp.float32
            )
            * inv_width
        ).astype(jnp.bfloat16)
        squeeze_sum = (
            squeeze_sum
            + lax.dot_general(
                saved, hidden_grad, (((0,), (0,)), ((), ())), preferred_element_type=jnp.float32
            )
            * inv_width
        )
        expand_sum = (
            expand_sum
            + lax.dot_general(
                regated, upstream, (((0,), (0,)), ((), ())), preferred_element_type=jnp.float32
            )
            * inv_rank
        )
        if tick + 1 < ticks:
            incoming_fwd = passed_along(layer_out, "pipe", 1)
            incoming_bwd = passed_along(downstream, "pipe", -1)
    return (
        squeeze_new[None],
        expand_new[None],
        squeeze_sum.astype(jnp.bfloat16)[None, None],
        expand_sum.astype(jnp.bfloat16)[None, None],
        layer_out[None, None],
        downstream[None, None],
    )


def solution(mesh):
    placed = (
        P("dp", "pipe", "mp"),
        P("dp", "pipe", "mp"),
        P("pipe", "mp", None),
        P("pipe", None, "mp"),
        P("dp", "pipe", "mp", None),
        P("dp", "pipe", None, "mp"),
        P("dp", "pipe", None, None, "mp"),
        P("dp", "pipe", None, "mp"),
        P("dp", "pipe", None, "mp"),
    )
    return jax.shard_map(
        shards,
        mesh=mesh,
        in_specs=placed,
        out_specs=(
            P("pipe", "mp", None),
            P("pipe", None, "mp"),
            P("dp", "pipe", "mp", None),
            P("dp", "pipe", None, "mp"),
            P("dp", "pipe", None, "mp"),
            P("dp", "pipe", None, "mp"),
        ),
        check_vma=False,
    )
```

profile of v0, /device:TPU:59, one launch (start us, length us, event | category | flops | bytes accessed | tf_op | source)
XLA Modules:
  0.0 370.3 jit_solution(3020351787675416026)
XLA Ops:
  7.2 0.8 copy.15
  8.0 65.3 %all_gather.6 = bf16[1,128,3584]{2,0,1:T(2,128)(2,1)S(1)} all-gather(bf16[1,4,3584]{2,0,1:T(2,128)(2,1)S(1)} %copy.15), channel_id=1, replica_groups=mesh['pipe'=32,'dp'=8,'mp'=2] {'pipe'}, dimensions={1}, use_global_device_ids=true | all-gather | bytes 946176 | tf_op jit(solution)/shard_map/all_gather | solution.py:61
  73.4 2.7 fusion.506
  76.1 72.3 %all_gather.7 = bf16[1,128,3584]{2,0,1:T(2,128)(2,1)S(1)} all-gather(bf16[1,4,3584]{2,0,1:T(2,128)(2,1)S(1)} %copy.17), channel_id=1, replica_groups=mesh['pipe'=32,'dp'=8,'mp'=2] {'pipe'}, dimensions={1}, use_global_device_ids=true | all-gather | bytes 946176 | tf_op jit(solution)/shard_map/all_gather | solution.py:62
  148.4 2.9 fusion.507
  152.2 1.1 fusion.79
  153.6 30.5 %all-reduce.7 = (f32[16,64]{1,0:T(8,128)S(1)}, f32[16,64]{1,0:T(8,128)S(1)}, f32[16,64]{1,0:T(8,128)S(1)}) all-reduce(f32[16,64]{1,0:T(8,128)S(1)} %fusion.39, f32[16,64]{1,0:T(8,128)S(1)} %fusion.79, f32[16,64]{1,0:T(8,128)S(1)} %fusion.77), channel_id=1, replica_groups=mesh['pipe'=32,'dp'=8,'mp'=2] {'mp'}, use_global_device_ids=true, to_apply=%region_2.3 | all-reduce | flops 3072 | bytes 24576 | tf_op jit(solution)/shard_map/psum | solution.py:93
  184.3 4.0 %collective-permute-start = (bf16[16,3584]{1,0:T(8,128)(2,1)S(1)}, bf16[16,3584]{1,0:T(8,128)(2,1)S(1)}, u32[]{:S(2)}, u32[]{:S(2)}) collective-permute-start(bf16[16,3584]{1,0:T(8,128)(2,1)S(1)} %fusion.13), channel_id=1, source_target_pairs={{0,16},{16,32},{32,48},{48,64},{64,80},{80,96},{96,112},{112,128},... | collective-permute-start | bytes 344072 | tf_op jit(solution)/shard_map/ppermute | solution.py:19
  188.5 3.4 collective-permute-start.1
  192.0 2.2 fusion.123
  194.5 2.3 collective-permute-done.1
  198.0 1.1 fusion.74
  199.1 4.2 %all-reduce.6 = (f32[16,64]{1,0:T(8,128)S(1)}, f32[16,64]{1,0:T(8,128)S(1)}, f32[16,64]{1,0:T(8,128)S(1)}) all-reduce(f32[16,64]{1,0:T(8,128)S(1)} %fusion.36, f32[16,64]{1,0:T(8,128)S(1)} %fusion.74, f32[16,64]{1,0:T(8,128)S(1)} %fusion.72), channel_id=1, replica_groups=mesh['pipe'=32,'dp'=8,'mp'=2] {'mp'}, use_global_device_ids=true, to_apply=%region_5.6 | all-reduce | flops 3072 | bytes 24576 | tf_op jit(solution)/shard_map/psum | solution.py:93
  203.6 1.6 convolution_add_fusion.8
  205.4 4.0 %collective-permute-start.2 = (bf16[16,3584]{1,0:T(8,128)(2,1)S(1)}, bf16[16,3584]{1,0:T(8,128)(2,1)S(1)}, u32[]{:S(2)}, u32[]{:S(2)}) collective-permute-start(bf16[16,3584]{1,0:T(8,128)(2,1)S(1)} %add_convert_fusion.13), channel_id=1, source_target_pairs={{0,16},{16,32},{32,48},{48,64},{64,80},{80,96},{96,112},{112,128},... | collective-permute-start | bytes 344072 | tf_op jit(solution)/shard_map/ppermute | solution.py:19
  209.4 3.4 collective-permute-start.3
  212.8 2.0 convolution_add_fusion.1
  214.8 3.5 collective-permute-done.3
  219.5 1.1 fusion.69
  220.7 6.3 %all-reduce.5 = (f32[16,64]{1,0:T(8,128)S(1)}, f32[16,64]{1,0:T(8,128)S(1)}, f32[16,64]{1,0:T(8,128)}) all-reduce(f32[16,64]{1,0:T(8,128)S(1)} %fusion.33, f32[16,64]{1,0:T(8,128)S(1)} %fusion.69, f32[16,64]{1,0:T(8,128)S(1)} %fusion.67), channel_id=1, replica_groups=mesh['pipe'=32,'dp'=8,'mp'=2] {'mp'}, use_global_device_ids=true, to_apply=%region_8.9 | all-reduce | flops 3072 | bytes 24576 | tf_op jit(solution)/shard_map/psum | solution.py:93
  227.8 1.3 convolution_add_fusion.7
  229.1 6.2 %collective-permute-start.5 = (bf16[16,3584]{1,0:T(8,128)(2,1)S(1)}, bf16[16,3584]{1,0:T(8,128)(2,1)S(1)}, u32[]{:S(2)}, u32[]{:S(2)}) collective-permute-start(bf16[16,3584]{1,0:T(8,128)(2,1)S(1)} %add_convert_fusion.10), channel_id=1, source_target_pairs={{16,0},{32,16},{48,32},{64,48},{80,64},{96,80},{112,96},{128,112},... | collective-permute-start | bytes 344072 | tf_op jit(solution)/shard_map/ppermute | solution.py:19
  235.5 1.9 collective-permute-start.4
  237.4 4.5 %collective-permute-done.5 = bf16[16,3584]{1,0:T(8,128)(2,1)S(1)} collective-permute-done((bf16[16,3584]{1,0:T(8,128)(2,1)S(1)}, bf16[16,3584]{1,0:T(8,128)(2,1)S(1)}, u32[]{:S(2)}, u32[]{:S(2)}) %collective-permute-start.5) | collective-permute-done | bytes 114720 | tf_op jit(solution)/shard_map/ppermute | solution.py:19
  242.1 6.6 %collective-permute-done.4 = bf16[16,3584]{1,0:T(8,128)(2,1)S(1)} collective-permute-done((bf16[16,3584]{1,0:T(8,128)(2,1)S(1)}, bf16[16,3584]{1,0:T(8,128)(2,1)S(1)}, u32[]{:S(2)}, u32[]{:S(2)}) %collective-permute-start.4) | collective-permute-done | bytes 114720 | tf_op jit(solution)/shard_map/ppermute | solution.py:19
  249.6 0.8 constant_dynamic-update-slice_fusion.11
  250.4 1.1 fusion.64
  251.5 5.1 %all-reduce.4 = (f32[16,64]{1,0:T(8,128)S(1)}, f32[16,64]{1,0:T(8,128)S(1)}, f32[16,64]{1,0:T(8,128)S(1)}) all-reduce(f32[16,64]{1,0:T(8,128)S(1)} %fusion.30, f32[16,64]{1,0:T(8,128)S(1)} %fusion.64, f32[16,64]{1,0:T(8,128)S(1)} %fusion.62), channel_id=1, replica_groups=mesh['pipe'=32,'dp'=8,'mp'=2] {'mp'}, use_global_device_ids=true, to_apply=%region_11.12 | all-reduce | flops 3072 | bytes 24576 | tf_op jit(solution)/shard_map/psum | solution.py:93
  256.7 1.2 fusion.316
  258.1 1.3 convolution_add_fusion.6
  259.6 1.9 collective-permute-start.6
  261.5 5.5 %collective-permute-start.7 = (bf16[16,3584]{1,0:T(8,128)(2,1)S(1)}, bf16[16,3584]{1,0:T(8,128)(2,1)S(1)}, u32[]{:S(2)}, u32[]{:S(2)}) collective-permute-start(bf16[16,3584]{1,0:T(8,128)(2,1)S(1)} %add_convert_fusion.8), channel_id=1, source_target_pairs={{16,0},{32,16},{48,32},{64,48},{80,64},{96,80},{112,96},{128,112},... | collective-permute-start | bytes 344072 | tf_op jit(solution)/shard_map/ppermute | solution.py:19
  267.7 0.8 constant_dynamic-update-slice_fusion.9
  270.4 0.8 bitcast_dynamic-update-slice_fusion.7
  271.2 1.2 fusion.59
  272.4 4.3 %all-reduce.3 = (f32[16,64]{1,0:T(8,128)S(1)}, f32[16,64]{1,0:T(8,128)S(1)}, f32[16,64]{1,0:T(8,128)S(1)}) all-reduce(f32[16,64]{1,0:T(8,128)S(1)} %fusion.27, f32[16,64]{1,0:T(8,128)S(1)} %fusion.59, f32[16,64]{1,0:T(8,128)S(1)} %fusion.57), channel_id=1, replica_groups=mesh['pipe'=32,'dp'=8,'mp'=2] {'mp'}, use_global_device_ids=true, to_apply=%region_14.15 | all-reduce | flops 3072 | bytes 24576 | tf_op jit(solution)/shard_map/psum | solution.py:93
  276.7 1.2 fusion.317
  278.2 1.3 convolution_add_fusion.5
  279.5 6.2 %collective-permute-start.9 = (bf16[16,3584]{1,0:T(8,128)(2,1)S(1)}, bf16[16,3584]{1,0:T(8,128)(2,1)S(1)}, u32[]{:S(2)}, u32[]{:S(2)}) collective-permute-start(bf16[16,3584]{1,0:T(8,128)(2,1)S(1)} %add_convert_fusion.6), channel_id=1, source_target_pairs={{16,0},{32,16},{48,32},{64,48},{80,64},{96,80},{112,96},{128,112},... | collective-permute-start | bytes 344072 | tf_op jit(solution)/shard_map/ppermute | solution.py:19
  285.9 1.9 collective-permute-start.8
  287.9 5.1 %collective-permute-done.9 = bf16[16,3584]{1,0:T(8,128)(2,1)S(1)} collective-permute-done((bf16[16,3584]{1,0:T(8,128)(2,1)S(1)}, bf16[16,3584]{1,0:T(8,128)(2,1)S(1)}, u32[]{:S(2)}, u32[]{:S(2)}) %collective-permute-start.9) | collective-permute-done | bytes 114720 | tf_op jit(solution)/shard_map/ppermute | solution.py:19
  293.2 5.1 %collective-permute-done.8 = bf16[16,3584]{1,0:T(8,128)(2,1)S(1)} collective-permute-done((bf16[16,3584]{1,0:T(8,128)(2,1)S(1)}, bf16[16,3584]{1,0:T(8,128)(2,1)S(1)}, u32[]{:S(2)}, u32[]{:S(2)}) %collective-permute-start.8) | collective-permute-done | bytes 114720 | tf_op jit(solution)/shard_map/ppermute | solution.py:19
  300.0 1.2 fusion.54
  301.1 5.4 %all-reduce.2 = (f32[16,64]{1,0:T(8,128)S(1)}, f32[16,64]{1,0:T(8,128)S(1)}, f32[16,64]{1,0:T(8,128)S(1)}) all-reduce(f32[16,64]{1,0:T(8,128)S(1)} %fusion.24, f32[16,64]{1,0:T(8,128)S(1)} %fusion.54, f32[16,64]{1,0:T(8,128)S(1)} %fusion.52), channel_id=1, replica_groups=mesh['pipe'=32,'dp'=8,'mp'=2] {'mp'}, use_global_device_ids=true, to_apply=%region_17.18 | all-reduce | flops 3072 | bytes 24576 | tf_op jit(solution)/shard_map/psum | solution.py:93
  306.8 2.1 collective-permute-start.10
  308.9 1.3 fusion.318
  310.1 1.3 convolution_add_fusion.4
  311.7 5.5 %collective-permute-start.11 = (bf16[16,3584]{1,0:T(8,128)(2,1)S(1)}, bf16[16,3584]{1,0:T(8,128)(2,1)S(1)}, u32[]{:S(2)}, u32[]{:S(2)}) collective-permute-start(bf16[16,3584]{1,0:T(8,128)(2,1)S(1)} %add_convert_fusion.4), channel_id=1, source_target_pairs={{16,0},{32,16},{48,32},{64,48},{80,64},{96,80},{112,96},{128,112},... | collective-permute-start | bytes 344072 | tf_op jit(solution)/shard_map/ppermute | solution.py:19
  317.2 3.7 collective-permute-done.10
  322.8 1.2 fusion.49
  324.0 5.0 %all-reduce.1 = (f32[16,64]{1,0:T(8,128)S(1)}, f32[16,64]{1,0:T(8,128)S(1)}, f32[16,64]{1,0:T(8,128)S(1)}) all-reduce(f32[16,64]{1,0:T(8,128)S(1)} %fusion.21, f32[16,64]{1,0:T(8,128)S(1)} %fusion.49, f32[16,64]{1,0:T(8,128)S(1)} %fusion.47), channel_id=1, replica_groups=mesh['pipe'=32,'dp'=8,'mp'=2] {'mp'}, use_global_device_ids=true, to_apply=%region_20.21 | all-reduce | flops 3072 | bytes 24576 | tf_op jit(solution)/shard_map/psum | solution.py:93
  329.0 1.3 fusion.319
  330.5 1.3 convolution_add_fusion.3
  331.8 7.0 %collective-permute-start.13 = (bf16[16,3584]{1,0:T(8,128)(2,1)S(1)}, bf16[16,3584]{1,0:T(8,128)(2,1)S(1)}, u32[]{:S(2)}, u32[]{:S(2)}) collective-permute-start(bf16[16,3584]{1,0:T(8,128)(2,1)S(1)} %add_convert_fusion.2), channel_id=1, source_target_pairs={{16,0},{32,16},{48,32},{64,48},{80,64},{96,80},{112,96},{128,112},... | collective-permute-start | bytes 344072 | tf_op jit(solution)/shard_map/ppermute | solution.py:19
  339.1 1.9 collective-permute-start.12
  341.5 5.9 %collective-permute-done.12 = bf16[16,3584]{1,0:T(8,128)(2,1)S(1)} collective-permute-done((bf16[16,3584]{1,0:T(8,128)(2,1)S(1)}, bf16[16,3584]{1,0:T(8,128)(2,1)S(1)}, u32[]{:S(2)}, u32[]{:S(2)}) %collective-permute-start.12) | collective-permute-done | bytes 114720 | tf_op jit(solution)/shard_map/ppermute | solution.py:19
  348.2 1.3 fusion.44
  349.5 4.6 %all-reduce = (f32[16,64]{1,0:T(8,128)S(1)}, f32[16,64]{1,0:T(8,128)S(1)}, f32[16,64]{1,0:T(8,128)S(1)}) all-reduce(f32[16,64]{1,0:T(8,128)S(1)} %fusion.18, f32[16,64]{1,0:T(8,128)S(1)} %fusion.44, f32[16,64]{1,0:T(8,128)S(1)} %fusion.42), channel_id=1, replica_groups=mesh['pipe'=32,'dp'=8,'mp'=2] {'mp'}, use_global_device_ids=true, to_apply=%region_23.24 | all-reduce | flops 3072 | bytes 24576 | tf_op jit(solution)/shard_map/psum | solution.py:93
  354.1 0.8 fusion.81
  355.0 0.8 fusion.82
  355.8 2.1 fusion.10
  358.3 1.3 fusion.9
  359.6 1.9 fusion.15
  361.5 1.9 fusion.16
  (115 shorter events, 16.6 us)
Async XLA Ops:
  7.2 352.4 %all-reduce.11.cloned.1.call-start = ((), (), s32[]{:S(2)}) async-start(), calls=%async_computation | async-start | bytes 1835008 | tf_op jit(solution)/shard_map/psum | solution.py:47
  73.4 2.7 copy-start.24
  148.4 2.9 copy-start.7
  148.4 3.5 copy-start
  151.3 2.0 copy-start.1
  151.3 2.0 copy-start.19
  184.3 12.8 %collective-permute-start = (bf16[16,3584]{1,0:T(8,128)(2,1)S(1)}, bf16[16,3584]{1,0:T(8,128)(2,1)S(1)}, u32[]{:S(2)}, u32[]{:S(2)}) collective-permute-start(bf16[16,3584]{1,0:T(8,128)(2,1)S(1)} %fusion.13), channel_id=1, source_target_pairs={{0,16},{16,32},{32,48},{48,64},{64,80},{80,96},{96,112},{112,128},... | collective-permute-start | bytes 344072 | tf_op jit(solution)/shard_map/ppermute | solution.py:19
  188.5 8.3 %collective-permute-start.1 = (bf16[16,3584]{1,0:T(8,128)(2,1)S(1)}, bf16[16,3584]{1,0:T(8,128)(2,1)S(1)}, u32[]{:S(2)}, u32[]{:S(2)}) collective-permute-start(bf16[16,3584]{1,0:T(8,128)(2,1)S(1)} %fusion.14), channel_id=1, source_target_pairs={{16,0},{32,16},{48,32},{64,48},{80,64},{96,80},{112,96},{128,112},... | collective-permute-start | bytes 344072 | tf_op jit(solution)/shard_map/ppermute | solution.py:19
  203.4 2.0 copy-start.22
  205.2 13.1 %copy-start.18 = (bf16[1,16,3584]{2,0,1:T(2,128)(2,1)S(1)}, bf16[1,16,3584]{2,0,1:T(2,128)(2,1)}, u32[]{:S(2)}) copy-start(bf16[1,16,3584]{2,0,1:T(2,128)(2,1)} %get-tuple-element.62) | copy-start | bytes 344068
  205.2 13.3 %copy-start.17 = (bf16[1,16,3584]{2,0,1:T(2,128)(2,1)S(1)}, bf16[1,16,3584]{2,0,1:T(2,128)(2,1)}, u32[]{:S(2)}) copy-start(bf16[1,16,3584]{2,0,1:T(2,128)(2,1)} %get-tuple-element.54) | copy-start | bytes 344068
  205.4 13.1 %collective-permute-start.2 = (bf16[16,3584]{1,0:T(8,128)(2,1)S(1)}, bf16[16,3584]{1,0:T(8,128)(2,1)S(1)}, u32[]{:S(2)}, u32[]{:S(2)}) collective-permute-start(bf16[16,3584]{1,0:T(8,128)(2,1)S(1)} %add_convert_fusion.13), channel_id=1, source_target_pairs={{0,16},{16,32},{32,48},{48,64},{64,80},{80,96},{96,112},{112,128},... | collective-permute-start | bytes 344072 | tf_op jit(solution)/shard_map/ppermute | solution.py:19
  209.4 8.9 %collective-permute-start.3 = (bf16[16,3584]{1,0:T(8,128)(2,1)S(1)}, bf16[16,3584]{1,0:T(8,128)(2,1)S(1)}, u32[]{:S(2)}, u32[]{:S(2)}) collective-permute-start(bf16[16,3584]{1,0:T(8,128)(2,1)S(1)} %add_convert_fusion.12), channel_id=1, source_target_pairs={{16,0},{32,16},{48,32},{64,48},{80,64},{96,80},{112,96},{128,112},... | collective-permute-start | bytes 344072 | tf_op jit(solution)/shard_map/ppermute | solution.py:19
  227.0 0.6 copy-start.20
  227.0 0.6 copy-start.23
  227.0 8.3 %copy-start.25 = (f32[16,64]{1,0:T(8,128)S(1)}, f32[16,64]{1,0:T(8,128)}, u32[]{:S(2)}) copy-start(f32[16,64]{1,0:T(8,128)} %get-tuple-element.23) | copy-start | bytes 12292
  227.0 14.9 %copy-start.16 = (bf16[1,16,3584]{2,0,1:T(2,128)(2,1)S(1)}, bf16[1,16,3584]{2,0,1:T(2,128)(2,1)}, u32[]{:S(2)}) copy-start(bf16[1,16,3584]{2,0,1:T(2,128)(2,1)} %get-tuple-element.61) | copy-start | bytes 344068
  229.1 12.9 %collective-permute-start.5 = (bf16[16,3584]{1,0:T(8,128)(2,1)S(1)}, bf16[16,3584]{1,0:T(8,128)(2,1)S(1)}, u32[]{:S(2)}, u32[]{:S(2)}) collective-permute-start(bf16[16,3584]{1,0:T(8,128)(2,1)S(1)} %add_convert_fusion.10), channel_id=1, source_target_pairs={{16,0},{32,16},{48,32},{64,48},{80,64},{96,80},{112,96},{128,112},... | collective-permute-start | bytes 344072 | tf_op jit(solution)/shard_map/ppermute | solution.py:19
  235.5 13.3 %collective-permute-start.4 = (bf16[16,3584]{1,0:T(8,128)(2,1)S(1)}, bf16[16,3584]{1,0:T(8,128)(2,1)S(1)}, u32[]{:S(2)}, u32[]{:S(2)}) collective-permute-start(bf16[16,3584]{1,0:T(8,128)(2,1)S(1)} %add_convert_fusion.11), channel_id=1, source_target_pairs={{0,16},{16,32},{32,48},{48,64},{64,80},{80,96},{96,112},{112,128},... | collective-permute-start | bytes 344072 | tf_op jit(solution)/shard_map/ppermute | solution.py:19
  258.1 11.2 %copy-start.15 = (bf16[1,16,3584]{2,0,1:T(2,128)(2,1)S(1)}, bf16[1,16,3584]{2,0,1:T(2,128)(2,1)}, u32[]{:S(2)}) copy-start(bf16[1,16,3584]{2,0,1:T(2,128)(2,1)} %get-tuple-element.60) | copy-start | bytes 344068
  259.4 10.1 %copy-start.14 = (bf16[1,16,3584]{2,0,1:T(2,128)(2,1)S(1)}, bf16[1,16,3584]{2,0,1:T(2,128)(2,1)}, u32[]{:S(2)}) copy-start(bf16[1,16,3584]{2,0,1:T(2,128)(2,1)} %get-tuple-element.52) | copy-start | bytes 344068
  259.6 9.9 %collective-permute-start.6 = (bf16[16,3584]{1,0:T(8,128)(2,1)S(1)}, bf16[16,3584]{1,0:T(8,128)(2,1)S(1)}, u32[]{:S(2)}, u32[]{:S(2)}) collective-permute-start(bf16[16,3584]{1,0:T(8,128)(2,1)S(1)} %add_convert_fusion.9), channel_id=1, source_target_pairs={{0,16},{16,32},{32,48},{48,64},{64,80},{80,96},{96,112},{112,128},... | collective-permute-start | bytes 344072 | tf_op jit(solution)/shard_map/ppermute | solution.py:19
  261.5 7.8 %collective-permute-start.7 = (bf16[16,3584]{1,0:T(8,128)(2,1)S(1)}, bf16[16,3584]{1,0:T(8,128)(2,1)S(1)}, u32[]{:S(2)}, u32[]{:S(2)}) collective-permute-start(bf16[16,3584]{1,0:T(8,128)(2,1)S(1)} %add_convert_fusion.8), channel_id=1, source_target_pairs={{16,0},{32,16},{48,32},{64,48},{80,64},{96,80},{112,96},{128,112},... | collective-permute-start | bytes 344072 | tf_op jit(solution)/shard_map/ppermute | solution.py:19
  278.0 15.0 %copy-start.13 = (bf16[1,16,3584]{2,0,1:T(2,128)(2,1)S(1)}, bf16[1,16,3584]{2,0,1:T(2,128)(2,1)}, u32[]{:S(2)}) copy-start(bf16[1,16,3584]{2,0,1:T(2,128)(2,1)} %get-tuple-element.59) | copy-start | bytes 344068
  278.2 20.2 %copy-start.12 = (bf16[1,16,3584]{2,0,1:T(2,128)(2,1)S(1)}, bf16[1,16,3584]{2,0,1:T(2,128)(2,1)}, u32[]{:S(2)}) copy-start(bf16[1,16,3584]{2,0,1:T(2,128)(2,1)} %get-tuple-element.51) | copy-start | bytes 344068
  279.5 13.5 %collective-permute-start.9 = (bf16[16,3584]{1,0:T(8,128)(2,1)S(1)}, bf16[16,3584]{1,0:T(8,128)(2,1)S(1)}, u32[]{:S(2)}, u32[]{:S(2)}) collective-permute-start(bf16[16,3584]{1,0:T(8,128)(2,1)S(1)} %add_convert_fusion.6), channel_id=1, source_target_pairs={{16,0},{32,16},{48,32},{64,48},{80,64},{96,80},{112,96},{128,112},... | collective-permute-start | bytes 344072 | tf_op jit(solution)/shard_map/ppermute | solution.py:19
  285.9 12.4 %collective-permute-start.8 = (bf16[16,3584]{1,0:T(8,128)(2,1)S(1)}, bf16[16,3584]{1,0:T(8,128)(2,1)S(1)}, u32[]{:S(2)}, u32[]{:S(2)}) collective-permute-start(bf16[16,3584]{1,0:T(8,128)(2,1)S(1)} %add_convert_fusion.7), channel_id=1, source_target_pairs={{0,16},{16,32},{32,48},{48,64},{64,80},{80,96},{96,112},{112,128},... | collective-permute-start | bytes 344072 | tf_op jit(solution)/shard_map/ppermute | solution.py:19
  306.8 14.1 %collective-permute-start.10 = (bf16[16,3584]{1,0:T(8,128)(2,1)S(1)}, bf16[16,3584]{1,0:T(8,128)(2,1)S(1)}, u32[]{:S(2)}, u32[]{:S(2)}) collective-permute-start(bf16[16,3584]{1,0:T(8,128)(2,1)S(1)} %add_convert_fusion.5), channel_id=1, source_target_pairs={{0,16},{16,32},{32,48},{48,64},{64,80},{80,96},{96,112},{112,128},... | collective-permute-start | bytes 344072 | tf_op jit(solution)/shard_map/ppermute | solution.py:19
  308.9 11.9 %copy-start.10 = (bf16[1,16,3584]{2,0,1:T(2,128)(2,1)S(1)}, bf16[1,16,3584]{2,0,1:T(2,128)(2,1)}, u32[]{:S(2)}) copy-start(bf16[1,16,3584]{2,0,1:T(2,128)(2,1)} %get-tuple-element.50) | copy-start | bytes 344068
  310.1 12.4 %copy-start.11 = (bf16[1,16,3584]{2,0,1:T(2,128)(2,1)S(1)}, bf16[1,16,3584]{2,0,1:T(2,128)(2,1)}, u32[]{:S(2)}) copy-start(bf16[1,16,3584]{2,0,1:T(2,128)(2,1)} %get-tuple-element.58) | copy-start | bytes 344068
  311.7 10.9 %collective-permute-start.11 = (bf16[16,3584]{1,0:T(8,128)(2,1)S(1)}, bf16[16,3584]{1,0:T(8,128)(2,1)S(1)}, u32[]{:S(2)}, u32[]{:S(2)}) collective-permute-start(bf16[16,3584]{1,0:T(8,128)(2,1)S(1)} %add_convert_fusion.4), channel_id=1, source_target_pairs={{16,0},{32,16},{48,32},{64,48},{80,64},{96,80},{112,96},{128,112},... | collective-permute-start | bytes 344072 | tf_op jit(solution)/shard_map/ppermute | solution.py:19
  330.3 11.0 %copy-start.9 = (bf16[1,16,3584]{2,0,1:T(2,128)(2,1)S(1)}, bf16[1,16,3584]{2,0,1:T(2,128)(2,1)}, u32[]{:S(2)}) copy-start(bf16[1,16,3584]{2,0,1:T(2,128)(2,1)} %get-tuple-element.57) | copy-start | bytes 344068
  330.5 16.9 %copy-start.8 = (bf16[1,16,3584]{2,0,1:T(2,128)(2,1)S(1)}, bf16[1,16,3584]{2,0,1:T(2,128)(2,1)}, u32[]{:S(2)}) copy-start(bf16[1,16,3584]{2,0,1:T(2,128)(2,1)} %get-tuple-element.49) | copy-start | bytes 344068
  331.8 9.4 %collective-permute-start.13 = (bf16[16,3584]{1,0:T(8,128)(2,1)S(1)}, bf16[16,3584]{1,0:T(8,128)(2,1)S(1)}, u32[]{:S(2)}, u32[]{:S(2)}) collective-permute-start(bf16[16,3584]{1,0:T(8,128)(2,1)S(1)} %add_convert_fusion.2), channel_id=1, source_target_pairs={{16,0},{32,16},{48,32},{64,48},{80,64},{96,80},{112,96},{128,112},... | collective-permute-start | bytes 344072 | tf_op jit(solution)/shard_map/ppermute | solution.py:19
  339.1 8.3 %collective-permute-start.12 = (bf16[16,3584]{1,0:T(8,128)(2,1)S(1)}, bf16[16,3584]{1,0:T(8,128)(2,1)S(1)}, u32[]{:S(2)}, u32[]{:S(2)}) collective-permute-start(bf16[16,3584]{1,0:T(8,128)(2,1)S(1)} %add_convert_fusion.3), channel_id=1, source_target_pairs={{0,16},{16,32},{32,48},{48,64},{64,80},{80,96},{96,112},{112,128},... | collective-permute-start | bytes 344072 | tf_op jit(solution)/shard_map/ppermute | solution.py:19
  348.2 10.0 %copy-start.6 = (f32[64,3584]{1,0:T(8,128)S(1)}, f32[64,3584]{1,0:T(8,128)}, u32[]{:S(2)}) copy-start(f32[64,3584]{1,0:T(8,128)} %fusion.319) | copy-start | bytes 2752516
  354.1 4.1 %copy-start.5 = (f32[64,3584]{1,0:T(8,128)S(1)}, f32[64,3584]{1,0:T(8,128)}, u32[]{:S(2)}) copy-start(f32[64,3584]{1,0:T(8,128)} %fusion.318) | copy-start | bytes 2752516
  354.9 3.3 copy-start.2
  354.9 3.3 copy-start.3
  354.9 3.3 copy-start.4
  354.9 3.3 copy-start.21
Sparse Core Ops, SparseCore 0:
  192.1 131.8 all-reduce.10
where the time goes:
time: 371 us; the launch traced here: 370 us
  blocking collectives  203 us (55%)
  starting transfers between devices  55 us (15%)
  matrix products  38.3 us (10%)
  waiting for transfers between devices  37.2 us (10%)
  between operations  14.6 us (4%)
  local copies, waits for them, and re-layouts  11.6 us (3%)
  other arithmetic  10.4 us (3%)
    all_gather x1, blocking collectives, shards(): lax.all_gather(cotangent, 'pipe', axis=1, tiled=True)  72.3 us
    psum x8, blocking collectives, shards(): again_total, grad_total = lax.psum((again_partial, grad_partial), 'mp')  65.5 us
    all_gather x1, blocking collectives, shards(): lax.all_gather(activations, 'pipe', axis=1, tiled=True)  65.3 us
    ppermute x14, starting transfers between devices, passed_along(): return lax.ppermute(block, axis, route)  54.9 us
    ppermute x14, waiting for transfers between devices, passed_along(): return lax.ppermute(block, axis, route)  37.2 us
    dot_general x8, matrix products, shards(): lax.dot_general(saved, hidden_grad, (((0,), (0,)), ((), ())), preferred_e...  12.4 us
    dot_general x8, matrix products, shards(): again_partial = jnp.dot(saved, squeeze, preferred_element_type=jnp.float32)  9.27 us
    dot_general x8, matrix products, shards(): lax.dot_general(regated, upstream, (((0,), (0,)), ((), ())), preferred_el...  8.9 us
  transfers between devices with their start and end apart: 15, of which 10 were waited for; matrix products, arithmetic and copies ran while one was open for 13% of the time, Pallas kernels for 0%

commit v1 on v0

v1 whole, which is shorter than its diff:
```python
import functools
import math

import jax
import jax.numpy as jnp
from jax import lax
from jax.experimental import pallas as pl
from jax.experimental.pallas import tpu as pltpu
from jax.sharding import PartitionSpec as P

D = 7168
RANK = 64
TICKS = 8
ROWS = 16
BRANCH_SCALE = 0.25
STEP_RATE = 0.5
CHUNKS = 2

F32 = jnp.float32
BF16 = jnp.bfloat16
MESH = pl.DeviceIdType.MESH
GELU_A = math.sqrt(2.0 / math.pi)
GELU_B = 0.044715


def gelu(v):
    return 0.5 * v * (1.0 + jnp.tanh(GELU_A * (v + GELU_B * (v * v * v))))


def gelu_slope(v):
    t = jnp.tanh(GELU_A * (v + GELU_B * (v * v * v)))
    inner = GELU_A * (1.0 + 3.0 * GELU_B * (v * v))
    return 0.5 * (1.0 + t) + 0.5 * v * ((1.0 - t * t) * inner)


def rows_by_rows(left, right):
    return lax.dot_general(left, right, (((1,), (1,)), ((), ())), preferred_element_type=F32)


def times(left, right):
    return jnp.dot(left, right, preferred_element_type=F32)


def window(
    sections, replicas, half,
    act, cot, sq, ex, lsq, lex, stash, fin, bin_,
    nsq, nex, gsq, gex, fco, bco,
    ss, ee, st, first, a_in, g_in, a_out, g_out, a_peer, g_peer, carry_peer,
    feed, feed_rows, again, again_peer, hg, rg, hg_peer, rg_peer, late, r1, p1, r2, p2, ry, new,
    grads, carry,
    load_sem, ss_send, ss_recv, first_send, first_recv, feed_send, feed_recv, again_send, again_recv,
    f_send, f_recv, b_send, b_recv, gp_send, gp_recv, ap_send, ap_recv, end_send, end_recv,
    late_send, late_recv, out_sem,
):
    width = half // CHUNKS
    inv_width = 1.0 / math.sqrt(D)
    inv_rank = BRANCH_SCALE / math.sqrt(RANK)
    s = lax.axis_index("pipe")
    dp = lax.axis_index("dp")
    c = lax.axis_index("mp")
    peer = 1 - c
    x = dp // 2
    yh = dp % 2
    x0 = x % 2
    x1 = x // 2
    x_one = (x + 1 - 2 * x0) * 2 + yh
    x_three = (3 - x) * 2 + yh
    y_other = x * 2 + 1 - yh
    is_first = s == 0
    is_last = s == sections - 1
    lag = 2 * sections - 1 - 2 * s
    late_section = lag < TICKS

    def remote(src, dst, send, recv, **where):
        return pltpu.make_async_remote_copy(
            src_ref=src, dst_ref=dst, send_sem=send, recv_sem=recv,
            device_id=where, device_id_type=MESH,
        )

    def landed(ref, sem):
        pltpu.make_async_copy(ref, ref, sem).wait()

    loads = [
        (fin, first.at[0, c]), (bin_, first.at[1, c]), (sq, ss.at[c]), (ex, ee.at[c]),
        (stash, st), (lsq, late.at[0]), (lex, late.at[1]),
    ]
    loads = [pltpu.make_async_copy(a, b, load_sem.at[i]) for i, (a, b) in enumerate(loads)]
    for load in loads:
        load.start()

    tick_of = s // 4
    feed_core = (s % 4) // 2
    feed_slot = c * 2 + s % 2
    own_feed = [is_first & (feed_core == c), is_last & (feed_core == c)]

    barrier = pltpu.get_barrier_semaphore()

    def hello(**where):
        pl.semaphore_signal(barrier, inc=1, device_id=where, device_id_type=MESH)

    hello(mp=peer)
    hello(dp=x_one)
    hello(dp=x_three)
    hello(dp=y_other)

    @pl.when(s > 0)
    def _():
        hello(pipe=s - 1)

    @pl.when(s < sections - 1)
    def _():
        hello(pipe=s + 1)

    for at_end in (is_first, is_last):
        @pl.when(at_end)
        def _():
            def greet(i, _):
                who = (i // 4) * 4 + 2 * c + (i // 2) % 2
                core = i % 2

                @pl.when((who != s) | (core != c))
                def _():
                    hello(pipe=who, mp=core)

                return 0

            lax.fori_loop(0, 4 * TICKS, greet, 0)

    expected = (
        4 + (s > 0).astype(jnp.int32) + (s < sections - 1).astype(jnp.int32)
        + 1 - own_feed[0].astype(jnp.int32) + 1 - own_feed[1].astype(jnp.int32)
    )
    pl.semaphore_wait(barrier, expected)

    firsts = [
        remote(src, first.at[i, c], first_send.at[i], first_recv.at[i], mp=peer)
        for i, src in enumerate((fin, bin_))
    ]
    weights = [
        remote(src, dst.at[c], ss_send.at[i], ss_recv.at[i], mp=peer)
        for i, (src, dst) in enumerate(((sq, ss), (ex, ee)))
    ]
    for copy in firsts + weights:
        copy.start()

    for k, (src, end) in enumerate(((act, 0), (cot, sections - 1))):
        @pl.when(own_feed[k])
        def _():
            pltpu.make_async_copy(
                src, feed.at[tick_of, feed_slot], feed_recv.at[tick_of, feed_slot]
            ).start()

        @pl.when(jnp.logical_not(own_feed[k]))
        def _():
            remote(
                src, feed.at[tick_of, feed_slot], feed_send.at[k],
                feed_recv.at[tick_of, feed_slot], pipe=end, mp=feed_core,
            ).start()

    b1 = (x0 + x1 - 2 * x0 * x1, x1)
    b2 = (x1, x0)
    near = (x_one, x_three)
    far = (x_three, x_one)
    sources = (lsq, lex)

    def rows(start, size):
        return pl.ds(pl.multiple_of(start, size), size)

    def late_copy(stage, h):
        sems = late_send.at[stage, h], late_recv.at[stage, h]
        if stage == 0:
            return remote(
                sources[h].at[rows(32 * (1 - b1[h]), 32)], r1.at[h], *sems, dp=near[h])
        if stage == 1:
            return remote(p1.at[h], r2.at[h], *sems, dp=far[h])
        if stage == 2:
            return remote(p2.at[h], ry.at[h], *sems, dp=y_other)
        if stage == 3:
            block = new.at[h, rows(32 * b1[h] + 16 * b2[h], 16)]
            return remote(block, block, *sems, dp=far[h])
        block = new.at[h, rows(32 * b1[h], 32)]
        return remote(block, block, *sems, dp=near[h])

    def late_landed(stage, h):
        if stage == 0:
            ref = r1.at[h]
        elif stage == 1:
            ref = r2.at[h]
        elif stage == 2:
            ref = ry.at[h]
        elif stage == 3:
            ref = new.at[h, rows(32 * b1[h] + 16 * (1 - b2[h]), 16)]
        else:
            ref = new.at[h, rows(32 * (1 - b1[h]), 32)]
        landed(ref, late_recv.at[stage, h])

    def late_step(stage, h):
        late_landed(stage, h)
        keep = rows(32 * b1[h] + 16 * b2[h], 16)
        give = rows(32 * b1[h] + 16 * (1 - b2[h]), 16)
        if stage == 0:
            p1[h] = (
                late[h, give, :].astype(F32) + r1[h, rows(16 * (1 - b2[h]), 16), :].astype(F32)
            ).astype(BF16)
        elif stage == 1:
            p2[h] = (
                late[h, keep, :].astype(F32) + r1[h, rows(16 * b2[h], 16), :].astype(F32)
                + r2[h].astype(F32)
            ).astype(BF16)
        elif stage == 2:
            total = p2[h].astype(F32) + ry[h].astype(F32)
            old = (ss, ee)[h][c, keep, :].astype(F32)
            new[h, keep, :] = (old - STEP_RATE * total / replicas).astype(BF16)
        if stage < 4:
            late_copy(stage + 1, h).start()

    for h in range(2):
        late_copy(0, h).start()

    for i in (2, 4):
        loads[i].wait()
    own_squeeze = ss[c]
    again[...] = rows_by_rows(st[...], jnp.concatenate([own_squeeze, own_squeeze], axis=0))
    again_copy = remote(again, again_peer, again_send, again_recv, mp=peer)
    again_copy.start()
    hg[...] = jnp.zeros_like(hg)
    rg[...] = jnp.zeros_like(rg)

    def crossed(w0, w1):
        w0 = w0.astype(F32)
        w1 = w1.astype(F32)
        low = jnp.concatenate([w0[:8], w1[:8]], axis=0)
        high = jnp.concatenate([w0[8:], w1[8:]], axis=0)
        return jnp.where(c == 0, low, high).astype(BF16)

    loads[0].wait()
    loads[1].wait()
    for i, (dst, at_end) in enumerate(((a_in, is_first), (g_in, is_last))):
        landed(first.at[i, peer], first_recv.at[i])
        for k in range(CHUNKS):
            cols = pl.ds(k * width, width)
            dst[0, k] = crossed(first[i, 0, :, cols], first[i, 1, :, cols])
    loads[3].wait()
    loads[5].wait()
    loads[6].wait()
    landed(ss.at[peer], ss_recv.at[0])
    landed(ee.at[peer], ss_recv.at[1])
    again_copy.wait()
    again[...] = (again[...] + again_peer[...]) * inv_width

    own_block = (lax.broadcasted_iota(jnp.int32, (ROWS, 2 * RANK), 0) < 8) == (
        lax.broadcasted_iota(jnp.int32, (ROWS, 2 * RANK), 1) < RANK
    )
    low_lanes = lax.broadcasted_iota(jnp.int32, (8, 2 * RANK), 1) < RANK

    def stacked(ref, k):
        return ref[:, :, pl.ds(k * width, width)].reshape(2 * RANK, width)

    def both(v):
        swapped = jnp.concatenate([v[8:], v[:8]], axis=0)
        return v + pltpu.roll(swapped, RANK, 1)

    def from_feed(tick, dst):
        for j in range(4):
            landed(feed.at[tick, j], feed_recv.at[tick, j])
        for j in range(4):
            feed_rows[pl.ds(4 * j, 4), :] = feed[tick, j].astype(F32)
        for k in range(CHUNKS):
            dst[tick, k] = feed_rows[:, pl.ds(k * width, width)].astype(BF16)

    def forward_copy(tick, k):
        return remote(
            a_out.at[tick, k], a_in.at[tick + 1, k], f_send.at[tick, k], f_recv.at[tick + 1, k],
            pipe=s + 1)

    def backward_copy(tick, k):
        return remote(
            g_out.at[tick, k], g_in.at[tick + 1, k], b_send.at[tick, k], b_recv.at[tick + 1, k],
            pipe=s - 1)

    def peer_copy(tick, src, dst, send, recv):
        return remote(src.at[tick], dst.at[tick], send.at[tick], recv.at[tick], mp=peer)

    def tick_body(tick, _):
        mine = pl.ds(pl.multiple_of(tick * ROWS + 8 * c, 8), 8)
        seen = again[mine, :]
        slope = gelu_slope(seen)
        rg[mine, :] = gelu(seen).astype(BF16).astype(F32)
        slope = jnp.concatenate([slope, slope], axis=0)

        @pl.when(is_first)
        def _():
            from_feed(tick, a_in)

        hidden = jnp.zeros((ROWS, 2 * RANK), F32)
        for k in range(CHUNKS):
            @pl.when(jnp.logical_not(is_first) & (tick > 0))
            def _():
                landed(a_in.at[tick, k], f_recv.at[tick, k])

            hidden = hidden + rows_by_rows(a_in[tick, k], stacked(ss, k))
        hidden = both(hidden) * inv_width
        gated = jnp.where(own_block, gelu(hidden), 0.0).astype(BF16)
        for k in range(CHUNKS):
            a_out[tick, k] = (
                a_in[tick, k].astype(F32) + times(gated, stacked(ee, k)) * inv_rank
            ).astype(BF16)

            @pl.when((tick < TICKS - 1) & (s < sections - 1))
            def _():
                forward_copy(tick, k).start()

        @pl.when(is_last)
        def _():
            from_feed(tick, g_in)

        gate_grad = jnp.zeros((ROWS, 2 * RANK), F32)
        for k in range(CHUNKS):
            @pl.when(jnp.logical_not(is_last) & (tick > 0))
            def _():
                landed(g_in.at[tick, k], b_recv.at[tick, k])

            gate_grad = gate_grad + rows_by_rows(g_in[tick, k], stacked(ee, k))
        gate_grad = both(gate_grad) * inv_rank
        hidden_grad = jnp.where(own_block, gate_grad * slope, 0.0).astype(BF16)
        for k in range(CHUNKS):
            g_out[tick, k] = (
                g_in[tick, k].astype(F32) + times(hidden_grad, stacked(ss, k)) * inv_width
            ).astype(BF16)

            @pl.when((tick < TICKS - 1) & (s > 0))
            def _():
                backward_copy(tick, k).start()

        hg[mine, :] = hidden_grad.astype(F32)[:8]
        peer_copy(tick, g_in, g_peer, gp_send, gp_recv).start()

        @pl.when(late_section)
        def _():
            peer_copy(tick, a_in, a_peer, ap_send, ap_recv).start()

            @pl.when(tick + lag < TICKS)
            def _():
                later = pl.ds(pl.multiple_of((tick + lag) * ROWS + 8 * c, 8), 8)
                again[later, :] = jnp.where(low_lanes, hidden[:8], hidden[8:])

        for stage, at in enumerate((1, 2, 5, 6)):
            @pl.when(tick == at)
            def _():
                for h in range(2):
                    late_step(stage, h)

        return 0

    lax.fori_loop(0, TICKS, tick_body, 0)

    ends = [
        remote(src, dst, end_send.at[i], end_recv.at[i], mp=peer)
        for i, (src, dst) in enumerate((
            (hg, hg_peer), (rg, rg_peer),
            (a_out.at[TICKS - 1], carry_peer.at[0]), (g_out.at[TICKS - 1], carry_peer.at[1]),
        ))
    ]
    for copy in ends:
        copy.start()
    ends[0].wait()
    ends[1].wait()

    def swapped_rows(v):
        v = v.reshape(TICKS, 2, 8, 2 * RANK)
        return jnp.concatenate([v[:, 1:], v[:, :1]], axis=1).reshape(TICKS * ROWS, 2 * RANK)

    def as_left(v):
        return jnp.transpose(v)[:RANK].astype(BF16)

    def all_ticks(ref, k):
        return ref[:, k].reshape(TICKS * ROWS, width)

    total_hg = hg[...] + hg_peer[...]
    row = lax.broadcasted_iota(jnp.int32, (TICKS * ROWS, 2 * RANK), 0)
    left = as_left(jnp.where(row < lag * ROWS, total_hg, 0.0))
    for k in range(CHUNKS):
        cols = pl.ds(k * width, width)
        grads[0, :, cols] = times(left, st[:, cols]) * inv_width

    @pl.when(late_section)
    def _():
        for tick in range(TICKS):
            peer_copy(tick, a_in, a_peer, ap_send, ap_recv).wait()
        moved = []
        for ref, swap in ((hg, False), (hg_peer, True)):
            pieces = []
            for tick in range(TICKS):
                source = jnp.minimum(tick + lag, TICKS - 1)
                piece = ref[pl.ds(pl.multiple_of(source * ROWS, ROWS), ROWS), :]
                if swap:
                    piece = jnp.concatenate([piece[8:], piece[:8]], axis=0)
                pieces.append(jnp.where(tick + lag < TICKS, piece, 0.0))
            moved.append(as_left(jnp.concatenate(pieces, axis=0)))
        for k in range(CHUNKS):
            cols = pl.ds(k * width, width)
            grads[0, :, cols] = grads[0, :, cols] + inv_width * (
                times(moved[0], all_ticks(a_in, k)) + times(moved[1], all_ticks(a_peer, k))
            )

    for tick in range(TICKS):
        peer_copy(tick, g_in, g_peer, gp_send, gp_recv).wait()
    own_left = as_left(rg[...])
    peer_left = as_left(swapped_rows(rg_peer[...]))
    for k in range(CHUNKS):
        cols = pl.ds(k * width, width)
        grads[1, :, cols] = inv_rank * (
            times(own_left, all_ticks(g_in, k)) + times(peer_left, all_ticks(g_peer, k))
        )
    gsq[...] = grads[0].astype(BF16)
    gex[...] = grads[1].astype(BF16)

    ends[2].wait()
    ends[3].wait()
    for i, (src, out) in enumerate(((a_out, fco), (g_out, bco))):
        for k in range(CHUNKS):
            mine = src[TICKS - 1, k].astype(F32)
            other = carry_peer[i, k].astype(F32)
            out[:, pl.ds(k * width, width)] = crossed(
                jnp.where(c == 0, mine, other), jnp.where(c == 0, other, mine))

    for h in range(2):
        late_landed(4, h)
    nsq[...] = new[0]
    nex[...] = new[1]

    for copy in firsts + weights:
        copy.wait_send()
    for k, (src, end) in enumerate(((act, 0), (cot, sections - 1))):
        @pl.when(jnp.logical_not(own_feed[k]))
        def _():
            remote(
                src, feed.at[tick_of, feed_slot], feed_send.at[k],
                feed_recv.at[tick_of, feed_slot], pipe=end, mp=feed_core,
            ).wait_send()
    for stage in range(5):
        for h in range(2):
            late_copy(stage, h).wait_send()

    def sent(tick, _):
        for k in range(CHUNKS):
            @pl.when(s < sections - 1)
            def _():
                forward_copy(tick, k).wait_send()

            @pl.when(s > 0)
            def _():
                backward_copy(tick, k).wait_send()

        return 0

    lax.fori_loop(0, TICKS - 1, sent, 0)


def shards(
    activations, cotangent, squeeze_old, expand_old, squeeze_late, expand_late,
    stash_inputs, forward_in, backward_in,
):
    sections = lax.axis_size("pipe")
    replicas = lax.axis_size("dp")
    half = squeeze_old.shape[1]
    width = half // CHUNKS
    vmem = pltpu.VMEM
    dma = pltpu.SemaphoreType.DMA
    ticked = vmem((TICKS, CHUNKS, ROWS, width), BF16)
    small = vmem((TICKS * ROWS, 2 * RANK), F32)
    any_spec = pl.BlockSpec(memory_space=pl.ANY)
    vmem_spec = pl.BlockSpec(memory_space=pltpu.VMEM)
    outs = pl.pallas_call(
        functools.partial(window, sections, replicas, half),
        out_shape=[jax.ShapeDtypeStruct((RANK, half), BF16)] * 4
        + [jax.ShapeDtypeStruct((ROWS, half), BF16)] * 2,
        in_specs=[any_spec] * 9,
        out_specs=[vmem_spec] * 6,
        scratch_shapes=[
            vmem((2, RANK, half), BF16),
            vmem((2, RANK, half), BF16),
            vmem((TICKS * ROWS, half), BF16),
            vmem((2, 2, ROWS, half), BF16),
            ticked, ticked, ticked, ticked, ticked, ticked,
            vmem((2, CHUNKS, ROWS, width), BF16),
            vmem((TICKS, 4, 4, half), BF16),
            vmem((ROWS, half), F32),
            small, small, small, small, small, small,
            vmem((2, RANK, half), BF16),
            vmem((2, 32, half), BF16),
            vmem((2, 16, half), BF16),
            vmem((2, 16, half), BF16),
            vmem((2, 16, half), BF16),
            vmem((2, 16, half), BF16),
            vmem((2, RANK, half), BF16),
            vmem((2, RANK, half), F32),
            vmem((8, 128), F32),
            dma((7,)),
            dma((2,)), dma((2,)),
            dma((2,)), dma((2,)),
            dma((2,)), dma((TICKS, 4)),
            dma, dma,
            dma((TICKS, CHUNKS)), dma((TICKS, CHUNKS)),
            dma((TICKS, CHUNKS)), dma((TICKS, CHUNKS)),
            dma((TICKS,)), dma((TICKS,)), dma((TICKS,)), dma((TICKS,)),
            dma((4,)), dma((4,)),
            dma((5, 2)), dma((5, 2)),
            dma((6,)),
        ],
        compiler_params=pltpu.CompilerParams(
            collective_id=0, has_side_effects=True, vmem_limit_bytes=48 * 1024 * 1024
        ),
        name="window",
    )(
        activations[0], cotangent[0], squeeze_old[0].T, expand_old[0],
        squeeze_late[0, 0].T, expand_late[0, 0], stash_inputs[0, 0].reshape(TICKS * ROWS, half),
        forward_in[0, 0], backward_in[0, 0],
    )
    nsq, nex, gsq, gex, fco, bco = outs
    return (
        nsq.T[None], nex[None], gsq.T[None, None], gex[None, None],
        fco[None, None], bco[None, None],
    )


def solution(mesh):
    placed = (
        P("dp", "pipe", "mp"),
        P("dp", "pipe", "mp"),
        P("pipe", "mp", None),
        P("pipe", None, "mp"),
        P("dp", "pipe", "mp", None),
        P("dp", "pipe", None, "mp"),
        P("dp", "pipe", None, None, "mp"),
        P("dp", "pipe", None, "mp"),
        P("dp", "pipe", None, "mp"),
    )
    return jax.shard_map(
        shards,
        mesh=mesh,
        in_specs=placed,
        out_specs=(
            P("pipe", "mp", None),
            P("pipe", None, "mp"),
            P("dp", "pipe", "mp", None),
            P("dp", "pipe", None, "mp"),
            P("dp", "pipe", None, "mp"),
            P("dp", "pipe", None, "mp"),
        ),
        check_vma=False,
    )
```

time: 371 us -> 86.4 us (0.23)
  the two profiles are of different devices: /device:TPU:59 before, /device:TPU:9 now
where the time goes in v1:
time: 86.4 us; the launch traced here: 85.4 us
  Pallas kernels  71.9 us (83%)
  local copies, waits for them, and re-layouts  12.9 us (15%)
    pallas_call x1, Pallas kernels, shards(): pl.pallas_call(functools.partial(window, sections, replicas, half), out_s...  71.9 us
    unnamed x24, local copies, waits for them, and re-layouts  12.9 us

profile of v1, /device:TPU:9, one launch (start us, length us, event | category | flops | bytes accessed | tf_op | source)
XLA Modules:
  0.0 85.4 jit_solution(8498405673123147369)
XLA Ops:
  0.6 0.0 copy-start
  0.6 1.2 %copy-done = bf16[1,1,8,16,3584]{4,3,2,1,0:T(8,128)(2,1)S(1)} copy-done((bf16[1,1,8,16,3584]{4,3,2,1,0:T(8,128)(2,1)S(1)}, bf16[1,1,8,16,3584]{4,3,2,1,0:T(8,128)(2,1)}, u32[]{:S(2)}) %copy-start) | copy-done | bytes 917528
  1.8 0.0 copy-start.1
  1.8 1.0 %copy-done.1 = bf16[1,3584,64]{1,2,0:T(8,128)(2,1)S(1)} copy-done((bf16[1,3584,64]{1,2,0:T(8,128)(2,1)S(1)}, bf16[1,3584,64]{1,2,0:T(8,128)(2,1)}, u32[]{:S(2)}) %copy-start.1) | copy-done | bytes 458776
  2.8 0.0 copy-start.2
  2.8 1.0 %copy-done.2 = bf16[1,64,3584]{2,1,0:T(8,128)(2,1)S(1)} copy-done((bf16[1,64,3584]{2,1,0:T(8,128)(2,1)S(1)}, bf16[1,64,3584]{2,1,0:T(8,128)(2,1)}, u32[]{:S(2)}) %copy-start.2) | copy-done | bytes 458776
  3.9 0.0 copy-start.3
  3.9 1.0 %copy-done.3 = bf16[1,1,3584,64]{2,3,1,0:T(8,128)(2,1)S(1)} copy-done((bf16[1,1,3584,64]{2,3,1,0:T(8,128)(2,1)S(1)}, bf16[1,1,3584,64]{2,3,1,0:T(8,128)(2,1)}, u32[]{:S(2)}) %copy-start.3) | copy-done | bytes 458776
  4.9 0.0 copy-start.4
  4.9 1.0 %copy-done.4 = bf16[1,1,64,3584]{3,2,1,0:T(8,128)(2,1)S(1)} copy-done((bf16[1,1,64,3584]{3,2,1,0:T(8,128)(2,1)S(1)}, bf16[1,1,64,3584]{3,2,1,0:T(8,128)(2,1)}, u32[]{:S(2)}) %copy-start.4) | copy-done | bytes 458776
  5.9 0.0 copy-start.5
  5.9 0.9 %copy-done.5 = bf16[1,1,16,3584]{3,2,1,0:T(8,128)(2,1)S(1)} copy-done((bf16[1,1,16,3584]{3,2,1,0:T(8,128)(2,1)S(1)}, bf16[1,1,16,3584]{3,2,1,0:T(8,128)(2,1)}, u32[]{:S(2)}) %copy-start.5) | copy-done | bytes 114712
  6.8 0.0 copy-start.6
  6.8 0.9 %copy-done.6 = bf16[1,1,16,3584]{3,2,1,0:T(8,128)(2,1)S(1)} copy-done((bf16[1,1,16,3584]{3,2,1,0:T(8,128)(2,1)S(1)}, bf16[1,1,16,3584]{3,2,1,0:T(8,128)(2,1)}, u32[]{:S(2)}) %copy-start.6) | copy-done | bytes 114712
  7.7 0.0 copy-start.7
  7.7 0.7 copy-done.7
  8.4 0.0 copy-start.8
  8.4 0.7 copy-done.8
  9.2 71.9 %window.1 = (bf16[64,3584]{1,0:T(8,128)(2,1)S(1)}, bf16[64,3584]{1,0:T(8,128)(2,1)S(1)}, bf16[64,3584]{1,0:T(8,128)(2,1)S(1)}, bf16[64,3584]{1,0:T(8,128)(2,1)S(...) custom-call(bf16[4,3584]{1,0:T(4,128)(2,1)S(1)} %bitcast.36, bf16[4,3584]{1,0:T(4,128)(2,1)S(1)} %bitcast.37, ...), custom_call_target="tpu_custom_call" | custom-call | tf_op jit(solution)/shard_map/window/pallas_call | solution.py:474
  81.1 0.8 copy.21
  81.8 0.8 copy.22
  82.6 0.8 copy.23
  83.4 0.8 copy.24
  84.1 0.6 copy.25
  84.8 0.6 copy.26
Async XLA Ops:
  0.6 1.2 %copy-start = (bf16[1,1,8,16,3584]{4,3,2,1,0:T(8,128)(2,1)S(1)}, bf16[1,1,8,16,3584]{4,3,2,1,0:T(8,128)(2,1)}, u32[]{:S(2)}) copy-start(bf16[1,1,8,16,3584]{4,3,2,1,0:T(8,128)(2,1)} %param.15) | copy-start | bytes 2752516
  1.8 1.0 %copy-start.1 = (bf16[1,3584,64]{1,2,0:T(8,128)(2,1)S(1)}, bf16[1,3584,64]{1,2,0:T(8,128)(2,1)}, u32[]{:S(2)}) copy-start(bf16[1,3584,64]{1,2,0:T(8,128)(2,1)} %param.11) | copy-start | bytes 1376260
  2.8 1.0 %copy-start.2 = (bf16[1,64,3584]{2,1,0:T(8,128)(2,1)S(1)}, bf16[1,64,3584]{2,1,0:T(8,128)(2,1)}, u32[]{:S(2)}) copy-start(bf16[1,64,3584]{2,1,0:T(8,128)(2,1)} %param.12) | copy-start | bytes 1376260
  3.9 1.0 %copy-start.3 = (bf16[1,1,3584,64]{2,3,1,0:T(8,128)(2,1)S(1)}, bf16[1,1,3584,64]{2,3,1,0:T(8,128)(2,1)}, u32[]{:S(2)}) copy-start(bf16[1,1,3584,64]{2,3,1,0:T(8,128)(2,1)} %param.13) | copy-start | bytes 1376260
  4.9 1.0 %copy-start.4 = (bf16[1,1,64,3584]{3,2,1,0:T(8,128)(2,1)S(1)}, bf16[1,1,64,3584]{3,2,1,0:T(8,128)(2,1)}, u32[]{:S(2)}) copy-start(bf16[1,1,64,3584]{3,2,1,0:T(8,128)(2,1)} %param.14) | copy-start | bytes 1376260
  5.9 0.9 %copy-start.5 = (bf16[1,1,16,3584]{3,2,1,0:T(8,128)(2,1)S(1)}, bf16[1,1,16,3584]{3,2,1,0:T(8,128)(2,1)}, u32[]{:S(2)}) copy-start(bf16[1,1,16,3584]{3,2,1,0:T(8,128)(2,1)} %param.16) | copy-start | bytes 344068
  6.8 0.9 %copy-start.6 = (bf16[1,1,16,3584]{3,2,1,0:T(8,128)(2,1)S(1)}, bf16[1,1,16,3584]{3,2,1,0:T(8,128)(2,1)}, u32[]{:S(2)}) copy-start(bf16[1,1,16,3584]{3,2,1,0:T(8,128)(2,1)} %param.17) | copy-start | bytes 344068
  7.7 0.7 copy-start.7
  8.4 0.7 copy-start.8

commit v2 on v1

v2 whole, which is shorter than its diff:
```python
import functools
import math

import jax
import jax.numpy as jnp
from jax import lax
from jax.experimental import pallas as pl
from jax.experimental.pallas import tpu as pltpu
from jax.sharding import PartitionSpec as P

D = 7168
RANK = 64
TICKS = 8
ROWS = 16
BRANCH_SCALE = 0.25
STEP_RATE = 0.5
GROUPS = 2
GROUP = 8
LATE_TICKS = ((1, 1), (2, 4), (3, 5))

F32 = jnp.float32
BF16 = jnp.bfloat16
MESH = pl.DeviceIdType.MESH
GELU_A = math.sqrt(2.0 / math.pi)
GELU_B = 0.044715


def gelu(v):
    return 0.5 * v * (1.0 + jnp.tanh(GELU_A * (v + GELU_B * (v * v * v))))


def gelu_slope(v):
    t = jnp.tanh(GELU_A * (v + GELU_B * (v * v * v)))
    inner = GELU_A * (1.0 + 3.0 * GELU_B * (v * v))
    return 0.5 * (1.0 + t) + 0.5 * v * ((1.0 - t * t) * inner)


def rows_by_rows(left, right):
    return lax.dot_general(left, right, (((1,), (1,)), ((), ())), preferred_element_type=F32)


def times(left, right):
    return jnp.dot(left, right, preferred_element_type=F32)


def window(
    sections, replicas, half,
    act, cot, sq, ex, lsq, lex, stash, fin, bin_,
    nsq, nex, gsq, gex, fco, bco,
    ss, ee, st, first, s_cols, e_cols, a_in, g_in, a_out, g_out, a_peer, g_peer, carry_peer,
    feed, feed_rows, again, again_peer, hg, rg, hg_peer, rg_peer, late, r1, p1, r2, p2, ry, new,
    grads, grads_out, carry,
    load_sem, ss_send, ss_recv, first_send, first_recv, feed_send, feed_recv, again_send, again_recv,
    f_send, f_recv, b_send, b_recv, gp_send, gp_recv, ap_send, ap_recv, end_send, end_recv,
    late_send, late_recv, out_sem,
):
    inv_width = 1.0 / math.sqrt(D)
    inv_rank = BRANCH_SCALE / math.sqrt(RANK)
    s = lax.axis_index("pipe")
    dp = lax.axis_index("dp")
    c = lax.axis_index("mp")
    peer = 1 - c
    x = dp // 2
    yh = dp % 2
    x0 = x % 2
    x1 = x // 2
    x_one = (x + 1 - 2 * x0) * 2 + yh
    x_three = (3 - x) * 2 + yh
    y_other = x * 2 + 1 - yh
    is_first = s == 0
    is_last = s == sections - 1
    lag = 2 * sections - 1 - 2 * s
    late_section = lag < TICKS

    def remote(src, dst, send, recv, **where):
        return pltpu.make_async_remote_copy(
            src_ref=src, dst_ref=dst, send_sem=send, recv_sem=recv,
            device_id=where, device_id_type=MESH,
        )

    def landed(ref, sem):
        pltpu.make_async_copy(ref, ref, sem).wait()

    loads = [
        (fin, first.at[0, c]), (bin_, first.at[1, c]), (sq, ss.at[c]), (ex, ee.at[c]),
        (stash, st), (lsq, late.at[0]), (lex, late.at[1]),
    ]
    loads = [pltpu.make_async_copy(a, b, load_sem.at[i]) for i, (a, b) in enumerate(loads)]
    for load in loads:
        load.start()

    feed_tick = s // 4
    feed_group = (s % 4) // 2
    feed_core = s % 2
    own_feed = [is_first & (feed_core == c), is_last & (feed_core == c)]

    barrier = pltpu.get_barrier_semaphore()

    def hello(**where):
        pl.semaphore_signal(barrier, inc=1, device_id=where, device_id_type=MESH)

    hello(mp=peer)
    hello(dp=x_one)
    hello(dp=x_three)
    hello(dp=y_other)

    @pl.when(s > 0)
    def _():
        hello(pipe=s - 1)

    @pl.when(s < sections - 1)
    def _():
        hello(pipe=s + 1)

    for at_end in (is_first, is_last):
        @pl.when(at_end)
        def _():
            def greet(i, _):
                who = (i // 2) * 2 + c
                core = i % 2

                @pl.when((who != s) | (core != c))
                def _():
                    hello(pipe=who, mp=core)

                return 0

            lax.fori_loop(0, sections, greet, 0)

    expected = (
        4 + (s > 0).astype(jnp.int32) + (s < sections - 1).astype(jnp.int32)
        + 1 - own_feed[0].astype(jnp.int32) + 1 - own_feed[1].astype(jnp.int32)
    )
    pl.semaphore_wait(barrier, expected)

    firsts = [
        remote(src, first.at[i, c], first_send.at[i], first_recv.at[i], mp=peer)
        for i, src in enumerate((fin, bin_))
    ]
    weights = [
        remote(src, dst.at[c], ss_send.at[i], ss_recv.at[i], mp=peer)
        for i, (src, dst) in enumerate(((sq, ss), (ex, ee)))
    ]
    for copy in firsts + weights:
        copy.start()

    def send_feed():
        for k, (src, end) in enumerate(((act, 0), (cot, sections - 1))):
            slot = feed.at[feed_tick, feed_group, c]
            sem = feed_recv.at[feed_tick, feed_group, c]

            @pl.when(own_feed[k])
            def _():
                pltpu.make_async_copy(src, slot, sem).start()

            @pl.when(jnp.logical_not(own_feed[k]))
            def _():
                remote(src, slot, feed_send.at[k], sem, pipe=end, mp=feed_core).start()

    pl.when(feed_tick < 2)(send_feed)

    b1 = (x0 + x1 - 2 * x0 * x1, x1)
    b2 = (x1, x0)
    near = (x_one, x_three)
    far = (x_three, x_one)
    sources = (lsq, lex)

    def rows(start, size):
        return pl.ds(pl.multiple_of(start, size), size)

    def late_copy(stage, h):
        sems = late_send.at[stage, h], late_recv.at[stage, h]
        if stage == 0:
            return remote(
                sources[h].at[rows(32 * (1 - b1[h]), 32)], r1.at[h], *sems, dp=near[h])
        if stage == 1:
            return remote(p1.at[h], r2.at[h], *sems, dp=far[h])
        if stage == 2:
            return remote(p2.at[h], ry.at[h], *sems, dp=y_other)
        if stage == 3:
            block = new.at[h, rows(32 * b1[h] + 16 * b2[h], 16)]
            return remote(block, block, *sems, dp=far[h])
        block = new.at[h, rows(32 * b1[h], 32)]
        return remote(block, block, *sems, dp=near[h])

    def late_landed(stage, h):
        if stage == 0:
            ref = r1.at[h]
        elif stage == 1:
            ref = r2.at[h]
        elif stage == 2:
            ref = ry.at[h]
        elif stage == 3:
            ref = new.at[h, rows(32 * b1[h] + 16 * (1 - b2[h]), 16)]
        else:
            ref = new.at[h, rows(32 * (1 - b1[h]), 32)]
        landed(ref, late_recv.at[stage, h])

    def late_step(stage, h):
        late_landed(stage, h)
        keep = rows(32 * b1[h] + 16 * b2[h], 16)
        give = rows(32 * b1[h] + 16 * (1 - b2[h]), 16)
        if stage == 0:
            p1[h] = (
                late[h, give, :].astype(F32) + r1[h, rows(16 * (1 - b2[h]), 16), :].astype(F32)
            ).astype(BF16)
        elif stage == 1:
            p2[h] = (
                late[h, keep, :].astype(F32) + r1[h, rows(16 * b2[h], 16), :].astype(F32)
                + r2[h].astype(F32)
            ).astype(BF16)
        elif stage == 2:
            total = p2[h].astype(F32) + ry[h].astype(F32)
            old = (ss, ee)[h][c, keep, :].astype(F32)
            new[h, keep, :] = (old - STEP_RATE * total / replicas).astype(BF16)
        if stage < 4:
            late_copy(stage + 1, h).start()

    for h in range(2):
        late_copy(0, h).start()

    for i in (2, 4):
        loads[i].wait()
    own_squeeze = ss[c]
    again[...] = rows_by_rows(st[...], jnp.concatenate([own_squeeze, own_squeeze], axis=0))
    again_copy = remote(again, again_peer, again_send, again_recv, mp=peer)
    again_copy.start()
    hg[...] = jnp.zeros_like(hg)
    rg[...] = jnp.zeros_like(rg)

    upper = lax.broadcasted_iota(jnp.int32, (GROUP, 2 * RANK), 0) < 4
    own_block = upper == (lax.broadcasted_iota(jnp.int32, (GROUP, 2 * RANK), 1) < RANK)
    own_rows = upper == (c == 0)
    upper_wide = lax.broadcasted_iota(jnp.int32, (GROUP, half), 0) < 4

    def crossed(w0, w1):
        w0 = w0.astype(F32)
        w1 = w1.astype(F32)
        low = jnp.where(upper_wide, w0, pltpu.roll(w1, 4, 0))
        high = jnp.where(upper_wide, pltpu.roll(w0, 4, 0), w1)
        return jnp.where(c == 0, low, high)

    loads[0].wait()
    loads[1].wait()
    for i, dst in enumerate((a_in, g_in)):
        landed(first.at[i, peer], first_recv.at[i])
        w0 = first[i, 0].astype(F32)
        w1 = first[i, 1].astype(F32)
        for g in range(GROUPS):
            mine = slice(GROUP * g, GROUP * (g + 1))
            dst[0, g] = crossed(w0[mine], w1[mine]).astype(BF16)
    loads[3].wait()
    loads[5].wait()
    loads[6].wait()
    landed(ss.at[peer], ss_recv.at[0])
    landed(ee.at[peer], ss_recv.at[1])

    def stacked(ref):
        return ref[...].reshape(2 * RANK, half)

    def both(v):
        return v + pltpu.roll(pltpu.roll(v, 4, 0), RANK, 1)

    def spread(v):
        return jnp.where(own_block, v, pltpu.roll(v, RANK, 1))

    def from_feed(tick, g, dst):
        for h in range(2):
            landed(feed.at[tick, g, h], feed_recv.at[tick, g, h])
        for h in range(2):
            feed_rows[pl.ds(4 * h, 4), :] = feed[tick, g, h].astype(F32)
        dst[tick, g] = feed_rows[pl.ds(0, GROUP), :].astype(BF16)

    def forward_copy(tick, g):
        return remote(
            a_out.at[tick, g], a_in.at[tick + 1, g], f_send.at[tick, g], f_recv.at[tick + 1, g],
            pipe=s + 1)

    def backward_copy(tick, g):
        return remote(
            g_out.at[tick, g], g_in.at[tick + 1, g], b_send.at[tick, g], b_recv.at[tick + 1, g],
            pipe=s - 1)

    def peer_copy(tick, src, dst, send, recv):
        return remote(src.at[tick], dst.at[tick], send.at[tick], recv.at[tick], mp=peer)

    def tile(tick, g):
        return pl.ds(pl.multiple_of(tick * ROWS + GROUP * g, GROUP), GROUP)

    def forward(tick, g, project):
        hidden = both(project(a_in[tick, g], ss, s_cols)) * inv_width
        gated = jnp.where(own_block, gelu(hidden), 0.0).astype(BF16)
        a_out[tick, g] = (
            a_in[tick, g].astype(F32) + times(gated, stacked(ee)) * inv_rank
        ).astype(BF16)

        @pl.when((tick < TICKS - 1) & (s < sections - 1))
        def _():
            forward_copy(tick, g).start()

        return hidden

    def keep_hidden(tick, g, hidden):
        @pl.when(tick + lag < TICKS)
        def _():
            again[tile(tick + lag, g), :] = spread(hidden)

    def backward(tick, g, slope, project):
        gate_grad = both(project(g_in[tick, g], ee, e_cols)) * inv_rank
        hidden_grad = jnp.where(own_block, gate_grad * slope, 0.0).astype(BF16)
        g_out[tick, g] = (
            g_in[tick, g].astype(F32) + times(hidden_grad, stacked(ss)) * inv_width
        ).astype(BF16)

        @pl.when((tick < TICKS - 1) & (s > 0))
        def _():
            backward_copy(tick, g).start()

        hg[tile(tick, g), :] = jnp.where(own_rows, spread(hidden_grad.astype(F32)), 0.0)

    def recomputed(tick, g):
        seen = again[tile(tick, g), :]
        seen = jnp.where(own_rows, seen, pltpu.roll(seen, 4, 0))
        rg[tile(tick, g), :] = jnp.where(own_rows, gelu(seen).astype(BF16).astype(F32), 0.0)
        return gelu_slope(seen)

    def after(tick):
        peer_copy(tick, g_in, g_peer, gp_send, gp_recv).start()

        @pl.when(late_section)
        def _():
            peer_copy(tick, a_in, a_peer, ap_send, ap_recv).start()

        @pl.when(feed_tick == tick + 2)
        def _():
            send_feed()

    def from_weights(v, ref, _):
        return rows_by_rows(v, stacked(ref))

    def from_columns(v, _, ref):
        return times(v, ref[...])

    hidden = [None] * GROUPS
    for g in range(GROUPS):
        @pl.when(is_first)
        def _():
            from_feed(0, g, a_in)

        hidden[g] = forward(0, g, from_weights)
    again_copy.wait()
    again[...] = (again[...] + again_peer[...]) * inv_width
    for g in range(GROUPS):
        keep_hidden(0, g, hidden[g])

        @pl.when(is_last)
        def _():
            from_feed(0, g, g_in)

        backward(0, g, recomputed(0, g), from_weights)
    after(0)
    for k in range(7):
        cols = pl.ds(k * (half // 7), half // 7)
        s_cols[cols, :] = jnp.transpose(ss[:, :, cols].reshape(2 * RANK, half // 7))
        e_cols[cols, :] = jnp.transpose(ee[:, :, cols].reshape(2 * RANK, half // 7))
    for h in range(2):
        late_step(0, h)

    def tick_body(tick, _):
        slopes = [recomputed(tick, g) for g in range(GROUPS)]
        for g in range(GROUPS):
            @pl.when(is_first)
            def _():
                from_feed(tick, g, a_in)

            @pl.when(jnp.logical_not(is_first))
            def _():
                landed(a_in.at[tick, g], f_recv.at[tick, g])

            keep_hidden(tick, g, forward(tick, g, from_columns))

            @pl.when(is_last)
            def _():
                from_feed(tick, g, g_in)

            @pl.when(jnp.logical_not(is_last))
            def _():
                landed(g_in.at[tick, g], b_recv.at[tick, g])

            backward(tick, g, slopes[g], from_columns)

        after(tick)
        for stage, at in LATE_TICKS:
            @pl.when(tick == at)
            def _():
                for h in range(2):
                    late_step(stage, h)

        return 0

    lax.fori_loop(1, TICKS, tick_body, 0)

    ends = [
        remote(src, dst, end_send.at[i], end_recv.at[i], mp=peer)
        for i, (src, dst) in enumerate((
            (hg, hg_peer), (rg, rg_peer),
            (a_out.at[TICKS - 1], carry_peer.at[0]), (g_out.at[TICKS - 1], carry_peer.at[1]),
        ))
    ]
    for copy in ends:
        copy.start()
    outs = []

    def put(src, dst):
        copy = pltpu.make_async_copy(src, dst, out_sem.at[len(outs)])
        copy.start()
        outs.append(copy)

    ends[0].wait()
    ends[1].wait()

    def swapped_rows(v):
        v = v.reshape(-1, 2, 4, 2 * RANK)
        return jnp.concatenate([v[:, 1:], v[:, :1]], axis=1).reshape(-1, 2 * RANK)

    def as_left(v):
        return jnp.transpose(v)[:RANK].astype(BF16)

    def all_ticks(ref):
        return ref[...].reshape(TICKS * ROWS, half)

    for tick in range(TICKS):
        peer_copy(tick, g_in, g_peer, gp_send, gp_recv).wait()
    grads_out[1] = (inv_rank * (
        times(as_left(rg[...]), all_ticks(g_in))
        + times(as_left(swapped_rows(rg_peer[...])), all_ticks(g_peer))
    )).astype(BF16)
    put(grads_out.at[1], gex)

    total_hg = hg[...] + hg_peer[...]
    row = lax.broadcasted_iota(jnp.int32, (TICKS * ROWS, 2 * RANK), 0)
    left = as_left(jnp.where(row < lag * ROWS, total_hg, 0.0))
    grads[...] = times(left, st[...])

    @pl.when(late_section)
    def _():
        for tick in range(TICKS):
            peer_copy(tick, a_in, a_peer, ap_send, ap_recv).wait()
        moved = []
        for ref, swap in ((hg, False), (hg_peer, True)):
            pieces = []
            for tick in range(TICKS):
                source = jnp.minimum(tick + lag, TICKS - 1)
                piece = ref[pl.ds(pl.multiple_of(source * ROWS, ROWS), ROWS), :]
                if swap:
                    piece = swapped_rows(piece)
                pieces.append(jnp.where(tick + lag < TICKS, piece, 0.0))
            moved.append(as_left(jnp.concatenate(pieces, axis=0)))
        grads[...] = (
            grads[...] + times(moved[0], all_ticks(a_in)) + times(moved[1], all_ticks(a_peer))
        )

    grads_out[0] = (inv_width * grads[...]).astype(BF16)
    put(grads_out.at[0], gsq)

    ends[2].wait()
    ends[3].wait()
    for i, (src, out) in enumerate(((a_out, fco), (g_out, bco))):
        for g in range(GROUPS):
            mine = src[TICKS - 1, g].astype(F32)
            other = carry_peer[i, g].astype(F32)
            feed_rows[pl.ds(GROUP * g, GROUP), :] = crossed(
                jnp.where(c == 0, mine, other), jnp.where(c == 0, other, mine))
        carry[i] = feed_rows[...].astype(BF16)
        put(carry.at[i], out)

    for h, out in enumerate((nsq, nex)):
        late_landed(4, h)
        put(new.at[h], out)

    for copy in firsts + weights:
        copy.wait_send()
    for k, (src, end) in enumerate(((act, 0), (cot, sections - 1))):
        @pl.when(jnp.logical_not(own_feed[k]))
        def _():
            remote(
                src, feed.at[feed_tick, feed_group, c], feed_send.at[k],
                feed_recv.at[feed_tick, feed_group, c], pipe=end, mp=feed_core,
            ).wait_send()
    for stage in range(5):
        for h in range(2):
            late_copy(stage, h).wait_send()

    def sent(tick, _):
        for g in range(GROUPS):
            @pl.when(s < sections - 1)
            def _():
                forward_copy(tick, g).wait_send()

            @pl.when(s > 0)
            def _():
                backward_copy(tick, g).wait_send()

        return 0

    lax.fori_loop(0, TICKS - 1, sent, 0)
    for copy in outs:
        copy.wait()


def put_out(*refs):
    sources, outs, held, sems = refs[:6], refs[6:12], refs[12:18], refs[18]
    ins = [pltpu.make_async_copy(a, b, sems.at[0, i]) for i, (a, b) in enumerate(zip(sources, held))]
    out = [pltpu.make_async_copy(a, b, sems.at[1, i]) for i, (a, b) in enumerate(zip(held, outs))]
    for copy in ins:
        copy.start()
    for first, second in zip(ins, out):
        first.wait()
        second.start()
    for copy in out:
        copy.wait()


def shards(
    activations, cotangent, squeeze_old, expand_old, squeeze_late, expand_late,
    stash_inputs, forward_in, backward_in,
):
    sections = lax.axis_size("pipe")
    replicas = lax.axis_size("dp")
    half = squeeze_old.shape[1]
    vmem = pltpu.VMEM
    dma = pltpu.SemaphoreType.DMA
    ticked = vmem((TICKS, GROUPS, GROUP, half), BF16)
    small = vmem((TICKS * ROWS, 2 * RANK), F32)
    hbm_spec = pl.BlockSpec(memory_space=pltpu.HBM)
    outs = pl.pallas_call(
        functools.partial(window, sections, replicas, half),
        out_shape=[jax.ShapeDtypeStruct((RANK, half), BF16)] * 4
        + [jax.ShapeDtypeStruct((ROWS, half), BF16)] * 2,
        in_specs=[hbm_spec] * 9,
        out_specs=[hbm_spec] * 6,
        scratch_shapes=[
            vmem((2, RANK, half), BF16),
            vmem((2, RANK, half), BF16),
            vmem((TICKS * ROWS, half), BF16),
            vmem((2, 2, ROWS, half), BF16),
            vmem((half, 2 * RANK), BF16),
            vmem((half, 2 * RANK), BF16),
            ticked, ticked, ticked, ticked, ticked, ticked,
            vmem((2, GROUPS, GROUP, half), BF16),
            vmem((TICKS, GROUPS, 2, 4, half), BF16),
            vmem((ROWS, half), F32),
            small, small, small, small, small, small,
            vmem((2, RANK, half), BF16),
            vmem((2, 32, half), BF16),
            vmem((2, 16, half), BF16),
            vmem((2, 16, half), BF16),
            vmem((2, 16, half), BF16),
            vmem((2, 16, half), BF16),
            vmem((2, RANK, half), BF16),
            vmem((RANK, half), F32),
            vmem((2, RANK, half), BF16),
            vmem((2, ROWS, half), BF16),
            dma((7,)),
            dma((2,)), dma((2,)),
            dma((2,)), dma((2,)),
            dma((2,)), dma((TICKS, GROUPS, 2)),
            dma, dma,
            dma((TICKS, GROUPS)), dma((TICKS, GROUPS)),
            dma((TICKS, GROUPS)), dma((TICKS, GROUPS)),
            dma((TICKS,)), dma((TICKS,)), dma((TICKS,)), dma((TICKS,)),
            dma((4,)), dma((4,)),
            dma((5, 2)), dma((5, 2)),
            dma((6,)),
        ],
        compiler_params=pltpu.CompilerParams(
            collective_id=0, has_side_effects=True, vmem_limit_bytes=62 * 1024 * 1024
        ),
        name="window",
    )(
        activations[0], cotangent[0], squeeze_old[0].T, expand_old[0],
        squeeze_late[0, 0].T, expand_late[0, 0], stash_inputs[0, 0].reshape(TICKS * ROWS, half),
        forward_in[0, 0], backward_in[0, 0],
    )
    nsq, nex, gsq, gex, fco, bco = pl.pallas_call(
        put_out,
        out_shape=[jax.ShapeDtypeStruct(out.shape, out.dtype) for out in outs],
        in_specs=[hbm_spec] * 6,
        out_specs=[hbm_spec] * 6,
        scratch_shapes=[vmem(out.shape, out.dtype) for out in outs] + [dma((2, 6))],
        compiler_params=pltpu.CompilerParams(vmem_limit_bytes=62 * 1024 * 1024),
        name="put_out",
    )(*outs)
    return (
        nsq.T[None], nex[None], gsq.T[None, None], gex[None, None],
        fco[None, None], bco[None, None],
    )


def solution(mesh):
    placed = (
        P("dp", "pipe", "mp"),
        P("dp", "pipe", "mp"),
        P("pipe", "mp", None),
        P("pipe", None, "mp"),
        P("dp", "pipe", "mp", None),
        P("dp", "pipe", None, "mp"),
        P("dp", "pipe", None, None, "mp"),
        P("dp", "pipe", None, "mp"),
        P("dp", "pipe", None, "mp"),
    )
    return jax.shard_map(
        shards,
        mesh=mesh,
        in_specs=placed,
        out_specs=(
            P("pipe", "mp", None),
            P("pipe", None, "mp"),
            P("dp", "pipe", "mp", None),
            P("dp", "pipe", None, "mp"),
            P("dp", "pipe", None, "mp"),
            P("dp", "pipe", None, "mp"),
        ),
        check_vma=False,
    )
```

time: 86.4 us -> 69.3 us (0.80)
  the two profiles are of different devices: /device:TPU:9 before, /device:TPU:17 now
where the time goes in v2:
time: 69.3 us; the launch traced here: 69.1 us
  Pallas kernels  68.5 us (99%)
    pallas_call x1, Pallas kernels, shards(): pl.pallas_call(functools.partial(window, sections, replicas, half), out_s...  66.1 us
    pallas_call x1, Pallas kernels, shards(): pl.pallas_call(put_out, out_shape=[jax.ShapeDtypeStruct(out.shape, out.dt...  2.41 us

profile of v2, /device:TPU:17, one launch (start us, length us, event | category | flops | bytes accessed | tf_op | source)
XLA Modules:
  0.0 69.1 jit_solution(2517103503799627739)
XLA Ops:
  0.6 66.1 %window.1 = (bf16[64,3584]{1,0:T(8,128)(2,1)}, bf16[64,3584]{1,0:T(8,128)(2,1)}, bf16[64,3584]{1,0:T(8,128)(2,1)}, bf16[64,3584]{1,0:T(8,128)(2,1)}, bf16[16,3584]{1,0:T(8,128)(2,1)}, /*index=5*/bf16[16,3584]{1,0:T(8,128)(2,1)}) custom-call(bf16[4,3584]{1,0:T(4,128)(2,1)} %bitcast.30, bf16[4,3584]{1,0:T(4,128)(2,1)} %bitcast.31, bf16[64,3584]{1,0:T(8,128)(2,1)} %bitcast.24, ...), custom_call_target="tpu_custom_call" | custom-call | tf_op jit(solution)/shard_map/window/pallas_call | solution.py:536
  66.7 2.4 %put_out.1 = (bf16[64,3584]{1,0:T(8,128)(2,1)}, bf16[64,3584]{1,0:T(8,128)(2,1)}, bf16[64,3584]{1,0:T(8,128)(2,1)}, bf16[64,3584]{1,0:T(8,128)(2,1)}, bf16[16,35...) custom-call(bf16[64,3584]{1,0:T(8,128)(2,1)} %get-tuple-element.18.refs_0_, bf16[64,3584]{1,0:T(8,128)(2,1)} %get-tuple-element.19.refs_1_, ...), custom_call_target="tpu_custom_call" | custom-call | tf_op jit(solution)/shard_map/put_out/pallas_call | solution.py:585

commit v3 on v2

v3 whole, which is shorter than its diff:
```python
import functools
import math

import jax
import jax.numpy as jnp
from jax import lax
from jax.experimental import pallas as pl
from jax.experimental.pallas import tpu as pltpu
from jax.sharding import PartitionSpec as P

D = 7168
RANK = 64
TICKS = 8
ROWS = 16
BRANCH_SCALE = 0.25
STEP_RATE = 0.5
GROUPS = 2
GROUP = 8
SUM_TICK = 1
EXCHANGE_TICKS = ((1, 2), (3, 4))
RENEW_TICKS = (4, 6)

F32 = jnp.float32
BF16 = jnp.bfloat16
MESH = pl.DeviceIdType.MESH
GELU_A = math.sqrt(2.0 / math.pi)
GELU_B = 0.044715


def gelu(v):
    return 0.5 * v * (1.0 + jnp.tanh(GELU_A * (v + GELU_B * (v * v * v))))


def gelu_slope(v):
    t = jnp.tanh(GELU_A * (v + GELU_B * (v * v * v)))
    inner = GELU_A * (1.0 + 3.0 * GELU_B * (v * v))
    return 0.5 * (1.0 + t) + 0.5 * v * ((1.0 - t * t) * inner)


def rows_by_rows(left, right):
    return lax.dot_general(left, right, (((1,), (1,)), ((), ())), preferred_element_type=F32)


def times(left, right):
    return jnp.dot(left, right, preferred_element_type=F32)


def window(
    sections, replicas, half,
    act, cot, sq, ex, lsq, lex, stash, fin, bin_,
    nsq, nex, gsq, gex, fco, bco,
    w, st, first, cols, x_in, x_out, x_peer, carry_peer, slopes,
    feed, feed_rows, again, again_peer, hg, rg, hg_peer, rg_peer, late, r1, p2, ry, new,
    grads, grads_out, carry,
    load_sem, ss_send, ss_recv, first_send, first_recv, feed_send, feed_recv, again_send, again_recv,
    x_send, x_recv, peer_send, peer_recv, end_send, end_recv,
    rs_send, rs_recv, y_send, y_recv, ag_send, ag_recv, out_sem,
):
    inv_width = 1.0 / math.sqrt(D)
    inv_rank = BRANCH_SCALE / math.sqrt(RANK)
    s = lax.axis_index("pipe")
    dp = lax.axis_index("dp")
    c = lax.axis_index("mp")
    peer = 1 - c
    x = dp // 2
    yh = dp % 2
    y_other = x * 2 + 1 - yh
    is_first = s == 0
    is_last = s == sections - 1
    lag = 2 * sections - 1 - 2 * s
    late_section = lag < TICKS

    def remote(src, dst, send, recv, **where):
        return pltpu.make_async_remote_copy(
            src_ref=src, dst_ref=dst, send_sem=send, recv_sem=recv,
            device_id=where, device_id_type=MESH,
        )

    def landed(ref, sem):
        pltpu.make_async_copy(ref, ref, sem).wait()

    loads = [
        (fin, first.at[0, c]), (bin_, first.at[1, c]), (sq, w.at[0, c]), (ex, w.at[1, c]),
        (stash, st), (lsq, late.at[0]), (lex, late.at[1]),
    ]
    loads = [pltpu.make_async_copy(a, b, load_sem.at[i]) for i, (a, b) in enumerate(loads)]
    for load in loads:
        load.start()

    feed_tick = s // 4
    feed_group = (s % 4) // 2
    feed_core = s % 2
    own_feed = [is_first & (feed_core == c), is_last & (feed_core == c)]

    barrier = pltpu.get_barrier_semaphore()

    def hello(**where):
        pl.semaphore_signal(barrier, inc=1, device_id=where, device_id_type=MESH)

    hello(mp=peer)
    for d in range(1, 4):
        hello(dp=((x + d) % 4) * 2 + yh)
    hello(dp=y_other)

    @pl.when(s > 0)
    def _():
        hello(pipe=s - 1)

    @pl.when(s < sections - 1)
    def _():
        hello(pipe=s + 1)

    for at_end in (is_first, is_last):
        @pl.when(at_end)
        def _():
            def greet(i, _):
                who = (i // 2) * 2 + c
                core = i % 2

                @pl.when((who != s) | (core != c))
                def _():
                    hello(pipe=who, mp=core)

                return 0

            lax.fori_loop(0, sections, greet, 0)

    expected = (
        5 + (s > 0).astype(jnp.int32) + (s < sections - 1).astype(jnp.int32)
        + 1 - own_feed[0].astype(jnp.int32) + 1 - own_feed[1].astype(jnp.int32)
    )
    pl.semaphore_wait(barrier, expected)

    firsts = [
        remote(src, first.at[i, c], first_send.at[i], first_recv.at[i], mp=peer)
        for i, src in enumerate((fin, bin_))
    ]
    weights = [
        remote(src, w.at[i, c], ss_send.at[i], ss_recv.at[i], mp=peer)
        for i, src in enumerate((sq, ex))
    ]
    for copy in firsts + weights:
        copy.start()

    def send_feed():
        for k, (src, end) in enumerate(((act, 0), (cot, sections - 1))):
            slot = feed.at[feed_tick, feed_group, c]
            sem = feed_recv.at[feed_tick, feed_group, c]

            @pl.when(own_feed[k])
            def _():
                pltpu.make_async_copy(src, slot, sem).start()

            @pl.when(jnp.logical_not(own_feed[k]))
            def _():
                remote(src, slot, feed_send.at[k], sem, pipe=end, mp=feed_core).start()

    pl.when(feed_tick < 2)(send_feed)

    sources = (lsq, lex)
    owned = pl.ds(pl.multiple_of(16 * x, 16), 16)

    def x_at(d):
        return (x + d) % 4

    def sixteen(d):
        return pl.ds(pl.multiple_of(16 * x_at(d), 16), 16)

    def spread_late(h, d):
        return remote(
            sources[h].at[sixteen(d)], r1.at[h, d - 1], rs_send.at[h, d - 1], rs_recv.at[h, d - 1],
            dp=x_at(d) * 2 + yh)

    def exchange_late(h, part):
        cols = pl.ds(part * (half // 2), half // 2)
        return remote(
            p2.at[h, :, cols], ry.at[h, :, cols], y_send.at[h, part], y_recv.at[h, part], dp=y_other)

    def share_new(h, d):
        block = new.at[h, owned]
        return remote(
            block, block, ag_send.at[h, d - 1], ag_recv.at[h, d - 1], dp=x_at(d) * 2 + yh)

    def sum_late(h):
        total = late[h, owned, :].astype(F32)
        for d in range(1, 4):
            landed(r1.at[h, d - 1], rs_recv.at[h, d - 1])
        for d in range(1, 4):
            total = total + r1[h, d - 1].astype(F32)
        p2[h] = total.astype(BF16)

    def renew(h):
        for part in range(2):
            cols = pl.ds(part * (half // 2), half // 2)
            landed(ry.at[h, :, cols], y_recv.at[h, part])
        total = p2[h].astype(F32) + ry[h].astype(F32)
        old = w[h, c, owned, :].astype(F32)
        new[h, owned, :] = (old - STEP_RATE * total / replicas).astype(BF16)
        for d in range(1, 4):
            share_new(h, d).start()

    for h in range(2):
        for d in range(1, 4):
            spread_late(h, d).start()

    for i in (2, 4):
        loads[i].wait()
    own_squeeze = w[0, c]
    again[...] = rows_by_rows(st[...], jnp.concatenate([own_squeeze, own_squeeze], axis=0))
    again_copy = remote(again, again_peer, again_send, again_recv, mp=peer)
    again_copy.start()
    hg[...] = jnp.zeros_like(hg)
    rg[...] = jnp.zeros_like(rg)

    upper = lax.broadcasted_iota(jnp.int32, (GROUP, 2 * RANK), 0) < 4
    own_block = upper == (lax.broadcasted_iota(jnp.int32, (GROUP, 2 * RANK), 1) < RANK)
    own_rows = upper == (c == 0)
    upper_wide = lax.broadcasted_iota(jnp.int32, (GROUP, half), 0) < 4

    def crossed(w0, w1):
        w0 = w0.astype(F32)
        w1 = w1.astype(F32)
        low = jnp.where(upper_wide, w0, pltpu.roll(w1, 4, 0))
        high = jnp.where(upper_wide, pltpu.roll(w0, 4, 0), w1)
        return jnp.where(c == 0, low, high)

    loads[0].wait()
    loads[1].wait()
    for i in range(2):
        landed(first.at[i, peer], first_recv.at[i])
        w0 = first[i, 0].astype(F32)
        w1 = first[i, 1].astype(F32)
        for g in range(GROUPS):
            mine = slice(GROUP * g, GROUP * (g + 1))
            x_in[i, 0, g] = crossed(w0[mine], w1[mine]).astype(BF16)
    loads[3].wait()
    for i in range(2):
        landed(w.at[i, peer], ss_recv.at[i])

    def stacked(i):
        return w[i].reshape(2 * RANK, half)

    def both(v):
        return v + pltpu.roll(pltpu.roll(v, 4, 0), RANK, 1)

    def spread(v):
        return jnp.where(own_block, v, pltpu.roll(v, RANK, 1))

    def from_feed(tick, g, d):
        for h in range(2):
            landed(feed.at[tick, g, h], feed_recv.at[tick, g, h])
        for h in range(2):
            feed_rows[pl.ds(4 * h, 4), :] = feed[tick, g, h].astype(F32)
        x_in[d, tick, g] = feed_rows[pl.ds(0, GROUP), :].astype(BF16)

    def goes_on(d, tick):
        to = s + 1 - 2 * d
        return (tick < TICKS - 1) & (to >= 0) & (to < sections)

    def hop(d, tick, g):
        return remote(
            x_out.at[d, tick, g], x_in.at[d, tick + 1, g],
            x_send.at[d, tick, g], x_recv.at[d, tick + 1, g], pipe=s + 1 - 2 * d)

    def peer_copy(d, tick):
        return remote(
            x_in.at[d, tick], x_peer.at[d, tick], peer_send.at[d, tick], peer_recv.at[d, tick],
            mp=peer)

    def tile(tick, g):
        return pl.ds(pl.multiple_of(tick * ROWS + GROUP * g, GROUP), GROUP)

    def keep_hidden(tick, g, value):
        again[tile(tick + lag, g), :] = spread(value)

    def chain(d, tick, g, product, slope, keep=True):
        forward = d == 0
        value = both(product) * jnp.where(forward, inv_width, inv_rank)
        middle = jnp.where(forward, gelu(value), value * slope)
        middle = jnp.where(own_block, middle, 0.0).astype(BF16)
        branch = times(middle, stacked(1 - d)) * jnp.where(forward, inv_rank, inv_width)
        x_out[d, tick, g] = (x_in[d, tick, g].astype(F32) + branch).astype(BF16)

        @pl.when(goes_on(d, tick))
        def _():
            hop(d, tick, g).start()

        if keep:
            @pl.when(forward & (tick + lag < TICKS))
            def _():
                keep_hidden(tick, g, value)

        @pl.when(d == 1)
        def _():
            hg[tile(tick, g), :] = jnp.where(own_rows, spread(middle.astype(F32)), 0.0)

        return value

    def recomputed(tick, g):
        seen = again[tile(tick, g), :]
        seen = jnp.where(own_rows, seen, pltpu.roll(seen, 4, 0))
        rg[tile(tick, g), :] = jnp.where(own_rows, gelu(seen).astype(BF16).astype(F32), 0.0)
        return gelu_slope(seen)

    def after(tick):
        peer_copy(1, tick).start()

        @pl.when(late_section)
        def _():
            peer_copy(0, tick).start()

        @pl.when(feed_tick == tick + 2)
        def _():
            send_feed()

    for g in range(GROUPS):
        @pl.when(is_first)
        def _():
            from_feed(0, g, 0)

        hidden = chain(0, 0, g, rows_by_rows(x_in[0, 0, g], stacked(0)), 0.0, keep=False)
        if g == 0:
            again_copy.wait()
            again[...] = (again[...] + again_peer[...]) * inv_width

        @pl.when(lag < TICKS)
        def _():
            keep_hidden(0, g, hidden)

        @pl.when(is_last)
        def _():
            from_feed(0, g, 1)

        chain(1, 0, g, rows_by_rows(x_in[1, 0, g], stacked(1)), recomputed(0, g))
    after(0)
    for k in range(7):
        some = pl.ds(k * (half // 7), half // 7)
        for i in range(2):
            cols[i, some, :] = jnp.transpose(w[i, :, :, some].reshape(2 * RANK, half // 7))
    loads[5].wait()
    loads[6].wait()

    rg_copy = remote(rg, rg_peer, end_send.at[1], end_recv.at[1], mp=peer)

    def tick_body(tick, _):
        for g in range(GROUPS):
            slopes[g] = recomputed(tick, g)
        @pl.when(tick == TICKS - 1)
        def _():
            rg_copy.start()

        for h in range(2):
            for part in range(2):
                @pl.when(tick == EXCHANGE_TICKS[h][part] + 1)
                def _():
                    exchange_late(h, part).start()

        turned = (s % 8 < tick).astype(jnp.int32)

        def slot(n, _):
            g = n // 2
            d = turned + (n % 2) * (1 - 2 * turned)
            fed = (is_first & (d == 0)) | (is_last & (d == 1))

            @pl.when(fed)
            def _():
                from_feed(tick, g, d)

            @pl.when(jnp.logical_not(fed))
            def _():
                landed(x_in.at[d, tick, g], x_recv.at[d, tick, g])

            chain(d, tick, g, times(x_in[d, tick, g], cols[d]), slopes[g])
            return 0

        lax.fori_loop(0, 2 * GROUPS, slot, 0)
        after(tick)
        @pl.when(tick == SUM_TICK)
        def _():
            for h in range(2):
                sum_late(h)

        for h in range(2):
            @pl.when(tick == RENEW_TICKS[h])
            def _():
                renew(h)

        return 0

    lax.fori_loop(1, TICKS, tick_body, 0)

    hg_copy = remote(hg, hg_peer, end_send.at[0], end_recv.at[0], mp=peer)
    carries = [
        remote(
            x_out.at[i, TICKS - 1], carry_peer.at[i], end_send.at[2 + i], end_recv.at[2 + i], mp=peer)
        for i in range(2)
    ]
    hg_copy.start()
    for copy in carries:
        copy.start()
    outs = []

    def put(src, dst):
        copy = pltpu.make_async_copy(src, dst, out_sem.at[len(outs)])
        copy.start()
        outs.append(copy)


    def swapped_rows(v):
        v = v.reshape(-1, 2, 4, 2 * RANK)
        return jnp.concatenate([v[:, 1:], v[:, :1]], axis=1).reshape(-1, 2 * RANK)

    def as_left(v):
        return jnp.transpose(v)[:RANK].astype(BF16)

    def all_ticks(ref):
        return ref.reshape(TICKS * ROWS, half)

    grads[...] = times(as_left(rg[...]), all_ticks(x_in[1]))
    rg_copy.wait()
    peer_left = as_left(swapped_rows(rg_peer[...]))
    for tick in range(TICKS):
        peer_copy(1, tick).wait()
    grads_out[1] = (inv_rank * (grads[...] + times(peer_left, all_ticks(x_peer[1])))).astype(BF16)
    put(grads_out.at[1], gex)

    hg_copy.wait()
    total_hg = hg[...] + hg_peer[...]
    row = lax.broadcasted_iota(jnp.int32, (TICKS * ROWS, 2 * RANK), 0)
    left = as_left(jnp.where(row < lag * ROWS, total_hg, 0.0))
    grads[...] = times(left, st[...])

    @pl.when(late_section)
    def _():
        for tick in range(TICKS):
            peer_copy(0, tick).wait()
        moved = []
        for ref, swap in ((hg, False), (hg_peer, True)):
            pieces = []
            for tick in range(TICKS):
                source = jnp.minimum(tick + lag, TICKS - 1)
                piece = ref[pl.ds(pl.multiple_of(source * ROWS, ROWS), ROWS), :]
                if swap:
                    piece = swapped_rows(piece)
                pieces.append(jnp.where(tick + lag < TICKS, piece, 0.0))
            moved.append(as_left(jnp.concatenate(pieces, axis=0)))
        grads[...] = (
            grads[...] + times(moved[0], all_ticks(x_in[0])) + times(moved[1], all_ticks(x_peer[0]))
        )

    grads_out[0] = (inv_width * grads[...]).astype(BF16)
    put(grads_out.at[0], gsq)

    for copy in carries:
        copy.wait()
    for i, out in enumerate((fco, bco)):
        for g in range(GROUPS):
            mine = x_out[i, TICKS - 1, g].astype(F32)
            other = carry_peer[i, g].astype(F32)
            feed_rows[pl.ds(GROUP * g, GROUP), :] = crossed(
                jnp.where(c == 0, mine, other), jnp.where(c == 0, other, mine))
        carry[i] = feed_rows[...].astype(BF16)
        put(carry.at[i], out)

    for h, out in enumerate((nsq, nex)):
        for d in range(1, 4):
            landed(new.at[h, sixteen(4 - d)], ag_recv.at[h, d - 1])
        put(new.at[h], out)

    for copy in firsts + weights:
        copy.wait_send()
    for k, (src, end) in enumerate(((act, 0), (cot, sections - 1))):
        @pl.when(jnp.logical_not(own_feed[k]))
        def _():
            remote(
                src, feed.at[feed_tick, feed_group, c], feed_send.at[k],
                feed_recv.at[feed_tick, feed_group, c], pipe=end, mp=feed_core,
            ).wait_send()
    for h in range(2):
        for d in range(1, 4):
            spread_late(h, d).wait_send()
            share_new(h, d).wait_send()
        for part in range(2):
            exchange_late(h, part).wait_send()

    def sent(tick, _):
        for g in range(GROUPS):
            for d in range(2):
                @pl.when(goes_on(d, tick))
                def _():
                    hop(d, tick, g).wait_send()

        return 0

    lax.fori_loop(0, TICKS - 1, sent, 0)
    for copy in outs:
        copy.wait()


def put_out(*refs):
    sources, outs, held, sems = refs[:6], refs[6:12], refs[12:18], refs[18]
    steps = []
    for i in range(6):
        size = 32 if i < 4 else 16
        for start in range(0, outs[i].shape[0], size):
            rows = pl.ds(start, size)
            n = len(steps)
            steps.append((
                pltpu.make_async_copy(sources[i].at[rows], held[i].at[rows], sems.at[0, n]),
                pltpu.make_async_copy(held[i].at[rows], outs[i].at[rows], sems.at[1, n]),
            ))
    for load, _ in steps:
        load.start()
    for load, store in steps:
        load.wait()
        store.start()
    for _, store in steps:
        store.wait()


def shards(
    activations, cotangent, squeeze_old, expand_old, squeeze_late, expand_late,
    stash_inputs, forward_in, backward_in,
):
    sections = lax.axis_size("pipe")
    replicas = lax.axis_size("dp")
    half = squeeze_old.shape[1]
    vmem = pltpu.VMEM
    dma = pltpu.SemaphoreType.DMA
    ticked = vmem((2, TICKS, GROUPS, GROUP, half), BF16)
    small = vmem((TICKS * ROWS, 2 * RANK), F32)
    hbm_spec = pl.BlockSpec(memory_space=pltpu.HBM)
    outs = pl.pallas_call(
        functools.partial(window, sections, replicas, half),
        out_shape=[jax.ShapeDtypeStruct((RANK, half), BF16)] * 4
        + [jax.ShapeDtypeStruct((ROWS, half), BF16)] * 2,
        in_specs=[hbm_spec] * 9,
        out_specs=[hbm_spec] * 6,
        scratch_shapes=[
            vmem((2, 2, RANK, half), BF16),
            vmem((TICKS * ROWS, half), BF16),
            vmem((2, 2, ROWS, half), BF16),
            vmem((2, half, 2 * RANK), BF16),
            ticked, ticked, ticked,
            vmem((2, GROUPS, GROUP, half), BF16),
            vmem((GROUPS, GROUP, 2 * RANK), F32),
            vmem((TICKS, GROUPS, 2, 4, half), BF16),
            vmem((ROWS, half), F32),
            small, small, small, small, small, small,
            vmem((2, RANK, half), BF16),
            vmem((2, 3, 16, half), BF16),
            vmem((2, 16, half), BF16),
            vmem((2, 16, half), BF16),
            vmem((2, RANK, half), BF16),
            vmem((RANK, half), F32),
            vmem((2, RANK, half), BF16),
            vmem((2, ROWS, half), BF16),
            dma((7,)),
            dma((2,)), dma((2,)),
            dma((2,)), dma((2,)),
            dma((2,)), dma((TICKS, GROUPS, 2)),
            dma, dma,
            dma((2, TICKS, GROUPS)), dma((2, TICKS, GROUPS)),
            dma((2, TICKS)), dma((2, TICKS)),
            dma((4,)), dma((4,)),
            dma((2, 3)), dma((2, 3)), dma((2, 2)), dma((2, 2)), dma((2, 3)), dma((2, 3)),
            dma((6,)),
        ],
        compiler_params=pltpu.CompilerParams(
            collective_id=0, has_side_effects=True, vmem_limit_bytes=62 * 1024 * 1024
        ),
        name="window",
    )(
        activations[0], cotangent[0], squeeze_old[0].T, expand_old[0],
        squeeze_late[0, 0].T, expand_late[0, 0], stash_inputs[0, 0].reshape(TICKS * ROWS, half),
        forward_in[0, 0], backward_in[0, 0],
    )
    nsq, nex, gsq, gex, fco, bco = pl.pallas_call(
        put_out,
        out_shape=[jax.ShapeDtypeStruct(out.shape, out.dtype) for out in outs],
        in_specs=[hbm_spec] * 6,
        out_specs=[hbm_spec] * 6,
        scratch_shapes=[vmem(out.shape, out.dtype) for out in outs] + [dma((2, 10))],
        compiler_params=pltpu.CompilerParams(vmem_limit_bytes=62 * 1024 * 1024),
        name="put_out",
    )(*outs)
    return (
        nsq.T[None], nex[None], gsq.T[None, None], gex[None, None],
        fco[None, None], bco[None, None],
    )


def solution(mesh):
    placed = (
        P("dp", "pipe", "mp"),
        P("dp", "pipe", "mp"),
        P("pipe", "mp", None),
        P("pipe", None, "mp"),
        P("dp", "pipe", "mp", None),
        P("dp", "pipe", None, "mp"),
        P("dp", "pipe", None, None, "mp"),
        P("dp", "pipe", None, "mp"),
        P("dp", "pipe", None, "mp"),
    )
    return jax.shard_map(
        shards,
        mesh=mesh,
        in_specs=placed,
        out_specs=(
            P("pipe", "mp", None),
            P("pipe", None, "mp"),
            P("dp", "pipe", "mp", None),
            P("dp", "pipe", None, "mp"),
            P("dp", "pipe", None, "mp"),
            P("dp", "pipe", None, "mp"),
        ),
        check_vma=False,
    )
```

time: 69.3 us -> 63.3 us (0.913)
  the two profiles are of different devices: /device:TPU:17 before, /device:TPU:9 now
where the time goes in v3:
time: 63.3 us; the launch traced here: 63.1 us
  Pallas kernels  62.5 us (99%)
  between operations  0.64 us (1%)
    pallas_call x1, Pallas kernels, shards(): pl.pallas_call(functools.partial(window, sections, replicas, half), out_s...  59.9 us
    pallas_call x1, Pallas kernels, shards(): pl.pallas_call(put_out, out_shape=[jax.ShapeDtypeStruct(out.shape, out.dt...  2.52 us

profile of v3, /device:TPU:9, one launch (start us, length us, event | category | flops | bytes accessed | tf_op | source)
XLA Modules:
  0.0 63.1 jit_solution(7769826364311893925)
XLA Ops:
  0.6 59.9 %window.1 = (bf16[64,3584]{1,0:T(8,128)(2,1)}, bf16[64,3584]{1,0:T(8,128)(2,1)}, bf16[64,3584]{1,0:T(8,128)(2,1)}, bf16[64,3584]{1,0:T(8,128)(2,1)}, bf16[16,3584]{1,0:T(8,128)(2,1)}, /*index=5*/bf16[16,3584]{1,0:T(8,128)(2,1)}) custom-call(bf16[4,3584]{1,0:T(4,128)(2,1)} %bitcast.30, bf16[4,3584]{1,0:T(4,128)(2,1)} %bitcast.31, bf16[64,3584]{1,0:T(8,128)(2,1)} %bitcast.24, ...), custom_call_target="tpu_custom_call" | custom-call | tf_op jit(solution)/shard_map/window/pallas_call | solution.py:533
  60.6 2.5 %put_out.1 = (bf16[64,3584]{1,0:T(8,128)(2,1)}, bf16[64,3584]{1,0:T(8,128)(2,1)}, bf16[64,3584]{1,0:T(8,128)(2,1)}, bf16[64,3584]{1,0:T(8,128)(2,1)}, bf16[16,35...) custom-call(bf16[64,3584]{1,0:T(8,128)(2,1)} %get-tuple-element.18.refs_0_, bf16[64,3584]{1,0:T(8,128)(2,1)} %get-tuple-element.19.refs_1_, ...), custom_call_target="tpu_custom_call" | custom-call | tf_op jit(solution)/shard_map/put_out/pallas_call | solution.py:578

commit v4 on v3

--- a/solution.py
+++ b/solution.py
@@ -79,51 +79,49 @@
     def landed(ref, sem):
         pltpu.make_async_copy(ref, ref, sem).wait()
 
+    feed_tick = s // 4
+    feed_group = (s % 4) // 2
+    feed_core = s % 2
+    own_feed = [is_first & (feed_core == c), is_last & (feed_core == c)]
+
+    barrier = pltpu.get_barrier_semaphore()
+
+    def hello(**where):
+        pl.semaphore_signal(barrier, inc=1, device_id=where, device_id_type=MESH)
+
+    for end, at_end in enumerate((is_first, is_last)):
+        @pl.when(at_end)
+        def _():
+            for i in range(sections):
+                who = (i // 2) * 2 + c
+                core = i % 2
+                if i == end * (sections - 1):
+                    @pl.when((who != s) | (core != c))
+                    def _():
+                        hello(pipe=who, mp=core)
+                else:
+                    hello(pipe=who, mp=core)
+
+    hello(mp=peer)
+    for d in range(1, 4):
+        hello(dp=((x + d) % 4) * 2 + yh)
+    hello(dp=y_other)
+
+    @pl.when(s > 0)
+    def _():
+        hello(pipe=s - 1)
+
+    @pl.when(s < sections - 1)
+    def _():
+        hello(pipe=s + 1)
+
     loads = [
         (fin, first.at[0, c]), (bin_, first.at[1, c]), (sq, w.at[0, c]), (ex, w.at[1, c]),
         (stash, st), (lsq, late.at[0]), (lex, late.at[1]),
     ]
     loads = [pltpu.make_async_copy(a, b, load_sem.at[i]) for i, (a, b) in enumerate(loads)]
-    for load in loads:
+    for load in loads[:5]:
         load.start()
-
-    feed_tick = s // 4
-    feed_group = (s % 4) // 2
-    feed_core = s % 2
-    own_feed = [is_first & (feed_core == c), is_last & (feed_core == c)]
-
-    barrier = pltpu.get_barrier_semaphore()
-
-    def hello(**where):
-        pl.semaphore_signal(barrier, inc=1, device_id=where, device_id_type=MESH)
-
-    hello(mp=peer)
-    for d in range(1, 4):
-        hello(dp=((x + d) % 4) * 2 + yh)
-    hello(dp=y_other)
-
-    @pl.when(s > 0)
-    def _():
-        hello(pipe=s - 1)
-
-    @pl.when(s < sections - 1)
-    def _():
-        hello(pipe=s + 1)
-
-    for at_end in (is_first, is_last):
-        @pl.when(at_end)
-        def _():
-            def greet(i, _):
-                who = (i // 2) * 2 + c
-                core = i % 2
-
-                @pl.when((who != s) | (core != c))
-                def _():
-                    hello(pipe=who, mp=core)
-
-                return 0
-
-            lax.fori_loop(0, sections, greet, 0)
 
     expected = (
         5 + (s > 0).astype(jnp.int32) + (s < sections - 1).astype(jnp.int32)
@@ -313,25 +311,36 @@
         def _():
             send_feed()
 
+    for load in loads[5:]:
+        load.start()
+
+    def first_product(d):
+        both_groups = [x_in[d, 0, g].astype(F32) for g in range(GROUPS)]
+        product = rows_by_rows(jnp.concatenate(both_groups, axis=0).astype(BF16), stacked(d))
+        return [product[GROUP * g:GROUP * (g + 1)] for g in range(GROUPS)]
+
     for g in range(GROUPS):
         @pl.when(is_first)
         def _():
             from_feed(0, g, 0)
 
-        hidden = chain(0, 0, g, rows_by_rows(x_in[0, 0, g], stacked(0)), 0.0, keep=False)
-        if g == 0:
-            again_copy.wait()
-            again[...] = (again[...] + again_peer[...]) * inv_width
-
-        @pl.when(lag < TICKS)
-        def _():
-            keep_hidden(0, g, hidden)
-
         @pl.when(is_last)
         def _():
             from_feed(0, g, 1)
 
-        chain(1, 0, g, rows_by_rows(x_in[1, 0, g], stacked(1)), recomputed(0, g))
+    product = first_product(0)
+    hidden = [chain(0, 0, g, product[g], 0.0, keep=False) for g in range(GROUPS)]
+    product = first_product(1)
+    again_copy.wait()
+    again[...] = (again[...] + again_peer[...]) * inv_width
+
+    @pl.when(lag < TICKS)
+    def _():
+        for g in range(GROUPS):
+            keep_hidden(0, g, hidden[g])
+
+    for g in range(GROUPS):
+        chain(1, 0, g, product[g], recomputed(0, g))
     after(0)
     for k in range(7):
         some = pl.ds(k * (half // 7), half // 7)
@@ -416,6 +425,12 @@
     def all_ticks(ref):
         return ref.reshape(TICKS * ROWS, half)
 
+    def put_new(h, out):
+        for d in range(1, 4):
+            landed(new.at[h, sixteen(4 - d)], ag_recv.at[h, d - 1])
+        put(new.at[h], out)
+
+    put_new(0, nsq)
     grads[...] = times(as_left(rg[...]), all_ticks(x_in[1]))
     rg_copy.wait()
     peer_left = as_left(swapped_rows(rg_peer[...]))
@@ -462,10 +477,7 @@
         carry[i] = feed_rows[...].astype(BF16)
         put(carry.at[i], out)
 
-    for h, out in enumerate((nsq, nex)):
-        for d in range(1, 4):
-            landed(new.at[h, sixteen(4 - d)], ag_recv.at[h, d - 1])
-        put(new.at[h], out)
+    put_new(1, nex)
 
     for copy in firsts + weights:
         copy.wait_send()

time: 63.3 us -> 62.9 us (level)
  no operation moved by 1% of the time
where the time goes in v4:
time: 62.9 us; the launch traced here: 62.7 us
  Pallas kernels  62.1 us (99%)
  between operations  0.64 us (1%)
    pallas_call x1, Pallas kernels, shards(): pl.pallas_call(functools.partial(window, sections, replicas, half), out_s...  59.5 us
    pallas_call x1, Pallas kernels, shards(): pl.pallas_call(put_out, out_shape=[jax.ShapeDtypeStruct(out.shape, out.dt...  2.52 us

profile of v4, /device:TPU:9, one launch (start us, length us, event | category | flops | bytes accessed | tf_op | source)
XLA Modules:
  0.0 62.7 jit_solution(17285243664095476391)
XLA Ops:
  0.6 59.5 %window.1 = (bf16[64,3584]{1,0:T(8,128)(2,1)}, bf16[64,3584]{1,0:T(8,128)(2,1)}, bf16[64,3584]{1,0:T(8,128)(2,1)}, bf16[64,3584]{1,0:T(8,128)(2,1)}, bf16[16,3584]{1,0:T(8,128)(2,1)}, /*index=5*/bf16[16,3584]{1,0:T(8,128)(2,1)}) custom-call(bf16[4,3584]{1,0:T(4,128)(2,1)} %bitcast.30, bf16[4,3584]{1,0:T(4,128)(2,1)} %bitcast.31, bf16[64,3584]{1,0:T(8,128)(2,1)} %bitcast.24, ...), custom_call_target="tpu_custom_call" | custom-call | tf_op jit(solution)/shard_map/window/pallas_call | solution.py:545
  60.2 2.5 %put_out.1 = (bf16[64,3584]{1,0:T(8,128)(2,1)}, bf16[64,3584]{1,0:T(8,128)(2,1)}, bf16[64,3584]{1,0:T(8,128)(2,1)}, bf16[64,3584]{1,0:T(8,128)(2,1)}, bf16[16,35...) custom-call(bf16[64,3584]{1,0:T(8,128)(2,1)} %get-tuple-element.18.refs_0_, bf16[64,3584]{1,0:T(8,128)(2,1)} %get-tuple-element.19.refs_1_, ...), custom_call_target="tpu_custom_call" | custom-call | tf_op jit(solution)/shard_map/put_out/pallas_call | solution.py:590
